TPU v7x, 128 devices: a whole 4x4x4 slice. The times are simulated.
128 devices in a mesh: replica: 32 (over y, z, x_hi), tensor: 4 (over x_lo, core).
Axes of the slice: x: 4 (x_hi: 2, x_lo: 2; x = x_hi * 2 + x_lo), y: 4, z: 4, core: 2. Of those that a mesh axis runs over, the one named last changes fastest.
Arguments:
- gate_pre: bfloat16 [32, 512, 7168], P('replica', None, 'tensor'), may hold values from -6 to 6
- up_pre: bfloat16 [32, 512, 7168], P('replica', None, 'tensor'), may hold values from -6 to 6
- down_weight: bfloat16 [32, 7168, 2560], P('replica', 'tensor'), may hold values from -6 to 6
- cotangent: bfloat16 [32, 512, 2560], P('replica', 'tensor'), may hold values from -6 to 6
- peer_exp: int32 [1], replicated, may hold values from 0 to 4
Outputs:
- layer_out: bfloat16 [32, 512, 2560], P('replica', 'tensor')
- grad_gate: bfloat16 [32, 512, 7168], P('replica', None, 'tensor')
- grad_up: bfloat16 [32, 512, 7168], P('replica', None, 'tensor')
- mixed_weight: bfloat16 [32, 7168, 2560], P('replica', 'tensor')
Inputs may be any that keep to these rules, and one draw needn't show every extreme that they name: `peer_exp`: one value for all replicas.
All inputs are finite; a program needn't handle non-finite values.
Results may differ from a plain program's by a relative error of at most 0.0052.
Values may be sent and summed in bfloat16 or wider, within the bound.
No kernel may reach another device: no remote copies, remote signals or barrier semaphores. Data moves between devices by JAX's collectives and lax.ppermute only.
A program may use at most 128 MiB of HBM per device.

v0:
```python
import jax
import jax.numpy as jnp
from jax import lax
from jax.sharding import PartitionSpec as P

learning_rate = 2.0


def as_sent(array):

    def short(part):
        return part.astype(jnp.bfloat16) if part.dtype == jnp.float32 else part

    return jax.tree.map(short, array)


def passed_along(value, axis, steps):
    count = lax.axis_size(axis)
    pairs = [(source, (source + steps) % count) for source in range(count)]
    return lax.ppermute(value, axis, pairs)


def contract_tokens(left, right):
    return lax.dot_general(
        left, right, (((0,), (0,)), ((), ())), preferred_element_type=jnp.float32
    )


def contract_width(left, right):
    return lax.dot_general(
        left, right, (((1,), (1,)), ((), ())), preferred_element_type=jnp.float32
    )


def peer_switch(payload, peer_exp, sender):
    replicas = lax.axis_size("replica")
    branches = []
    for power in range(5):
        distance = 2**power % replicas
        branches.append(partial_sender(sender, distance))
    return lax.switch(jnp.clip(peer_exp[0], 0, 4), branches, payload)


def partial_sender(sender, distance):

    def send(value):
        return sender(value, distance)

    return send


def send_updated(value, distance):
    return jax.tree.map(
        lambda part, own: part.astype(own.dtype),
        passed_along(as_sent(value), "replica", distance),
        value,
    )


def per_device(gate_pre, up_pre, down_weight, cotangent, peer_exp):
    gate = gate_pre[0].astype(jnp.float32)
    upv = up_pre[0].astype(jnp.float32)
    weight = down_weight[0]
    cot_rows = cotangent[0]
    width_all = weight.shape[0] * lax.axis_size("tensor")
    scale = 1.0 / jnp.sqrt(jnp.float32(width_all))
    sig = jax.nn.sigmoid(gate)
    act = gate * sig
    hidden = (act * upv).astype(jnp.bfloat16)
    piece = hidden
    layer_out = lax.psum_scatter(
        jnp.dot(piece, weight, preferred_element_type=jnp.float32) * scale,
        "tensor",
        scatter_dimension=0,
        tiled=True,
    ).astype(jnp.bfloat16)
    piece = lax.all_gather(cot_rows, "tensor", axis=0, tiled=True)
    weight_sum = contract_tokens(hidden, piece)
    grad_hidden = contract_width(piece, weight) * scale
    weight_sum, grad_hidden = (weight_sum, grad_hidden)
    updated = (weight.astype(jnp.float32) - learning_rate * scale * weight_sum).astype(jnp.bfloat16)
    peer_updated = peer_switch(updated, peer_exp, send_updated)
    grad_gate = (grad_hidden * upv * sig * (1.0 + gate * (1.0 - sig))).astype(jnp.bfloat16)
    grad_up = (grad_hidden * act).astype(jnp.bfloat16)
    mixed_weight = ((updated.astype(jnp.float32) + peer_updated.astype(jnp.float32)) * 0.5).astype(
        jnp.bfloat16
    )
    return (layer_out[None], grad_gate[None], grad_up[None], mixed_weight[None])


def solution(mesh):
    return jax.shard_map(
        per_device,
        mesh=mesh,
        in_specs=(
            P("replica", None, "tensor"),
            P("replica", None, "tensor"),
            P("replica", "tensor", None),
            P("replica", "tensor", None),
            P(),
        ),
        out_specs=(
            P("replica", "tensor", None),
            P("replica", None, "tensor"),
            P("replica", None, "tensor"),
            P("replica", "tensor", None),
        ),
        check_vma=False,
    )
```

profile of v0, /device:TPU:1, one launch (start us, length us, event | category | flops | bytes accessed | tf_op | source)
XLA Modules:
  0.0 337.2 jit_solution(11192155614801682167)
XLA Ops:
  7.2 0.0 all-gather.3.cloned.1.call-start
  7.2 0.7 all-gather.3.cloned.1.call-update
  7.9 0.0 reduce-scatter.2.cloned.1.call-start
  7.9 12.2 %fusion.8 = f32[512,2560]{1,0:T(8,128)} fusion(bf16[1,1792,2560]{2,1,0:T(8,128)(2,1)} %param.12, bf16[1,512,1792]{2,1,0:T(8,128)(2,1)} %param.11, bf16[1,512,1792]{2,1,0:T(8,128)(2,1)} %param.10), kind=kOutput, calls=%fused_computation.13 | convolution fusion | flops 4706271232 | bytes 18087936 | tf_op jit(solution)/shard_map/dot_general | solution.py:72
  20.2 0.0 copy-start.2
  20.2 0.0 reduce-scatter.2.cloned.1.call-update
  21.0 25.8 %all-gather.3.cloned.1.call-done = bf16[1,512,2560]{2,1,0:T(8,128)(2,1)} async-done(((bf16[1,128,2560]{2,1,0:T(8,128)(2,1)}), bf16[1,512,2560]{2,1,0:T(8,128)(2,1)}) %all-gather.3.cloned.1.call-update) | async-done | bytes 2621456 | tf_op jit(solution)/shard_map/all_gather | solution.py:77
  46.8 0.0 copy-done.2
  46.8 11.0 %subtract_convert_fusion = bf16[1792,2560]{1,0:T(8,128)(2,1)S(1)} fusion(bf16[1,1792,2560]{2,1,0:T(8,128)(2,1)} %param.12, bf16[1,512,2560]{2,1,0:T(8,128)(2,1)} %all-gather.3.cloned.1.call-done, bf16[1,512,1792]{2,1,0:T(8,128)(2,1)S(1)} %copy-done.2, bf16[1,512,1792]{2,1,0:T(8,128)(2,1)} %param.10), kind=kOutput, calls=%fused_computation.1 | convolution fusion | flops 4723310592 | bytes 24641536 | tf_op jit(solution)/shard_map/dot_general | solution.py:24
  57.8 0.0 copy-start
  57.8 3.9 %copy-done = bf16[1792,2560]{1,0:T(8,128)(2,1)} copy-done((bf16[1792,2560]{1,0:T(8,128)(2,1)}, bf16[1792,2560]{1,0:T(8,128)(2,1)S(1)}, u32[]{:S(2)}) %copy-start) | copy-done | bytes 9175064
  61.7 243.5 %conditional.4 = (bf16[1792,2560]{1,0:T(8,128)(2,1)}) conditional(s32[]{:T(128)} %bitcast.8, bf16[1792,2560]{1,0:T(8,128)(2,1)S(1)} %subtract_convert_fusion, bf16[1792,2560]{1,0:T(8,128)(2,1)S(1)} %subtract_convert_fusion, bf16[1792,2560]{1,0:T(8,128)(2,1)S(1)} %subtract_convert_fusion, ...), branch_computations={%region_1.2_spmd, %region_2.3_spmd, %region_3.4_spmd, %region_4.5_... | conditional | bytes 36700208
  61.7 2.5 collective-permute-start
  64.2 241.0 %collective-permute-done = bf16[1792,2560]{1,0:T(8,128)(2,1)} collective-permute-done((bf16[1792,2560]{1,0:T(8,128)(2,1)S(1)}, bf16[1792,2560]{1,0:T(8,128)(2,1)}, u32[]{:S(2)}, u32[]{:S(2)}) %collective-permute-start) | collective-permute-done | bytes 9175072 | tf_op jit(solution)/shard_map/cond/branch_0_fun/ppermute | solution.py:20
  305.2 0.0 copy-start.1
  305.2 12.9 %fusion.27 = (bf16[1,512,1792]{2,1,0:T(8,128)(2,1)}, bf16[1,512,1792]{2,1,0:T(8,128)(2,1)}) fusion(bf16[1,512,1792]{2,1,0:T(8,128)(2,1)} %param.10, bf16[1,512,1792]{2,1,0:T(8,128)(2,1)S(1)} %copy-done.2, bf16[1,1792,2560]{2,1,0:T(8,128)(2,1)} %param.12, bf16[1,512,2560]{2,1,0:T(8,128)(2,1)} %all-gather.3.cloned.1.call-done), kind=kOutput, calls=%fused_computation.33 | convolution fusion | flops 4712300544 | bytes 19136512 | tf_op jit(solution)/shard_map/dot_general | solution.py:30
  318.1 0.0 copy-done.1
  318.1 10.1 %fusion = bf16[1,1792,2560]{2,1,0:T(8,128)(2,1)} fusion(bf16[1792,2560]{1,0:T(8,128)(2,1)} %get-tuple-element.23, bf16[1792,2560]{1,0:T(8,128)(2,1)S(1)} %copy-done.1), kind=kLoop, calls=%fused_computation.2 | loop fusion | flops 22937600 | bytes 27525120 | tf_op jit(solution)/shard_map/broadcast_in_dim | solution.py:88
  328.2 0.0 reduce-scatter.2.cloned.1.call-done
  328.2 2.2 convert_bitcast_fusion.2
Async XLA Ops:
  7.2 39.6 %all-gather.3.cloned.1.call-start = ((), (), s32[]{:S(2)}) async-start(), calls=%async_computation.2 | async-start | bytes 3276800 | tf_op jit(solution)/shard_map/all_gather | solution.py:77
  7.9 320.3 %reduce-scatter.2.cloned.1.call-start = ((), (), s32[]{:S(2)}) async-start(), calls=%async_computation.1 | async-start | bytes 6553600 | tf_op jit(solution)/shard_map/reduce_scatter | solution.py:71
  20.2 26.6 %copy-start.2 = (bf16[1,512,1792]{2,1,0:T(8,128)(2,1)S(1)}, bf16[1,512,1792]{2,1,0:T(8,128)(2,1)}, u32[]{:S(2)}) copy-start(bf16[1,512,1792]{2,1,0:T(8,128)(2,1)} %param.11) | copy-start | bytes 5505028
  57.8 3.9 %copy-start = (bf16[1792,2560]{1,0:T(8,128)(2,1)}, bf16[1792,2560]{1,0:T(8,128)(2,1)S(1)}, u32[]{:S(2)}) copy-start(bf16[1792,2560]{1,0:T(8,128)(2,1)S(1)} %subtract_convert_fusion) | copy-start | bytes 27525124
  61.7 243.5 %collective-permute-start = (bf16[1792,2560]{1,0:T(8,128)(2,1)S(1)}, bf16[1792,2560]{1,0:T(8,128)(2,1)}, u32[]{:S(2)}, u32[]{:S(2)}) collective-permute-start(bf16[1792,2560]{1,0:T(8,128)(2,1)S(1)} %param), channel_id=1, source_target_pairs={{0,4},{4,8},{8,12},{12,16},{16,20},{20,24},{24,28},{28,32},{32,36}... | collective-permute-start | bytes 27525128 | tf_op jit(solution)/shard_map/cond/branch_0_fun/ppermute | solution.py:20
  305.2 12.9 %copy-start.1 = (bf16[1792,2560]{1,0:T(8,128)(2,1)S(1)}, bf16[1792,2560]{1,0:T(8,128)(2,1)}, u32[]{:S(2)}) copy-start(bf16[1792,2560]{1,0:T(8,128)(2,1)} %copy-done) | copy-start | bytes 27525124
Sparse Core Ops, SparseCore 0:
  9.7 37.0 all-gather.2
  49.2 92.0 reduce-scatter.1
where the time goes:
time: 337 us
  waiting for transfers between devices  267 us (79%)
  matrix products  36.1 us (11%)
  between operations  14.8 us (4%)
  other arithmetic  12.3 us (4%)
  local copies, waits for them, and re-layouts  3.93 us (1%)
    ppermute x1, waiting for transfers between devices, passed_along(): return lax.ppermute(value, axis, pairs)  241 us
    all_gather x1, waiting for transfers between devices, per_device(): piece = lax.all_gather(cot_rows, 'tensor', axis=0, tiled=True)  25.8 us
    dot_general x1, matrix products, contract_width(): lax.dot_general(left, right, (((1,), (1,)), ((), ())), preferred_element_...  12.9 us
    broadcast_in_dim x2, other arithmetic, per_device(): return (layer_out[None], grad_gate[None], grad_up[None], mixed_weight[None])  12.3 us
    dot_general x1, matrix products, per_device(): jnp.dot(piece, weight, preferred_element_type=jnp.float32) * scale  12.2 us
    dot_general x1, matrix products, contract_tokens(): lax.dot_general(left, right, (((0,), (0,)), ((), ())), preferred_element_...  11 us
  transfers between devices with their start and end apart: 3, of which 2 were waited for; matrix products, arithmetic and copies ran while one was open for 14% of the time, Pallas kernels for 0%

commit v1 on v0

v1 whole, which is shorter than its diff:
```python
import functools

import jax
import jax.numpy as jnp
import numpy as np
from jax import lax
from jax.experimental import pallas as pl
from jax.experimental.pallas import tpu as pltpu
from jax.sharding import PartitionSpec as P

learning_rate = 2.0
both = ("replica", "tensor")
vmem = 56 * 2**20
head = 768
head_cuts = (256, 256, 256)
even_cuts = (768, 512, 512)
odd_cuts = (384, 384, 512, 512)
cost_cut = 100
grads_wide = 256
params = pltpu.CompilerParams(vmem_limit_bytes=vmem)


def place(x, y, z, core):
    replica = (y % 4) * 8 + (z % 4) * 2 + (x % 4) // 2
    return replica * 4 + (x % 2) * 2 + core


def chips():
    return [(x, y, z, core) for x in range(4) for y in range(4) for z in range(4) for core in range(2)]


def direct_pairs(power):
    distance = 2**power
    return [
        (r * 4 + t, ((r + distance) % 32) * 4 + t) for r in range(32) for t in range(4)
    ]


def backward_hops(power):
    if power == 3:
        step = [(place(x, y, z, c), place(x, y - 1, z, c)) for x, y, z, c in chips()]
        return [step, step, step]
    step = [(place(x, y, z, c), place(x, y, z - 1, c)) for x, y, z, c in chips()]
    last = [
        (place(x, y, z, c), place(x, y + (1 if z == 1 else 0), z - 1, c))
        for x, y, z, c in chips()
    ]
    return [step, step, last]


def swapped(value, mask):
    return lax.ppermute(value, "tensor", [(t, t ^ mask) for t in range(4)])


def estimate(flops, read):
    return pl.CostEstimate(flops=flops // cost_cut, bytes_accessed=read // cost_cut, transcendentals=0)


def in_rows(count, step, body):
    def one(i, carry):
        body(pl.ds(pl.multiple_of(i * step, step), step))
        return carry

    lax.fori_loop(0, count // step, one, 0)


def hidden_kernel(gate_ref, up_ref, hidden_ref):
    def body(rows):
        gate = gate_ref[rows, :].astype(jnp.float32)
        up = up_ref[rows, :].astype(jnp.float32)
        hidden_ref[rows, :] = (gate * jax.nn.sigmoid(gate) * up).astype(jnp.bfloat16)

    in_rows(gate_ref.shape[0], 64, body)


def make_hidden(gate, up):
    tokens, units = gate.shape
    block = pl.BlockSpec((tokens, units // 2), lambda i: (0, i))
    return pl.pallas_call(
        hidden_kernel,
        grid=(2,),
        in_specs=[block, block],
        out_specs=block,
        out_shape=jax.ShapeDtypeStruct((tokens, units), jnp.bfloat16),
        compiler_params=params,
        cost_estimate=estimate(tokens * units * 10, tokens * units * 6),
    )(gate, up)


def put_tokens(at_ref, part_refs, whole_ref, lo):
    size, wide = part_refs[0].shape
    for mask, part in enumerate(part_refs):
        row = pl.multiple_of((at_ref[0] ^ mask) * size, size)
        whole_ref[pl.ds(row, size), lo : lo + wide] = part[...]


def updated_kernel(factor, first, cuts, at_ref, own, core, chip, far, hidden_ref, weight_ref, *refs):
    out_refs, cot_ref = refs[:-1], refs[-1]

    @pl.when(pl.program_id(0) == 0)
    def _():
        put_tokens(at_ref, (own, core, chip, far), cot_ref, 0)

    at = 0
    for out_ref, width in zip(out_refs, cuts):
        total = lax.dot_general(
            hidden_ref[...],
            cot_ref[:, at : at + width],
            (((0,), (0,)), ((), ())),
            preferred_element_type=jnp.float32,
        )
        old = weight_ref[:, first + at : first + at + width].astype(jnp.float32)
        out_ref[...] = (old - factor * total).astype(jnp.bfloat16)
        at += width


def make_updated(at, parts, hidden, weight, factor, first, cuts):
    tokens, units = hidden.shape
    rows = units // 2 if first == 0 else 256
    wide = sum(cuts)
    columns = wide if first == 0 else weight.shape[1]
    part = pl.BlockSpec(parts[0].shape, lambda i, at: (0, 0))
    return pl.pallas_call(
        functools.partial(updated_kernel, factor, first, cuts),
        grid_spec=pltpu.PrefetchScalarGridSpec(
            num_scalar_prefetch=1,
            grid=(units // rows,),
            in_specs=[part] * 4
            + [
                pl.BlockSpec((tokens, rows), lambda i, at: (0, i)),
                pl.BlockSpec((rows, columns), lambda i, at: (i, 0)),
            ],
            out_specs=[pl.BlockSpec((rows, width), lambda i, at: (i, 0)) for width in cuts],
            scratch_shapes=[pltpu.VMEM((tokens, wide), jnp.bfloat16)],
        ),
        out_shape=[jax.ShapeDtypeStruct((units, width), jnp.bfloat16) for width in cuts],
        compiler_params=params,
        cost_estimate=estimate(2 * units * tokens * wide, units * (columns + wide) * 2),
    )(at, *parts, hidden, weight)


def terms_kernel(scale, at_ref, hidden_ref, weight_ref, keep_ref, send_ref, total_ref):
    def body(rows):
        total_ref[rows, :] = scale * jnp.dot(
            hidden_ref[rows, :], weight_ref[...], preferred_element_type=jnp.float32
        )

    in_rows(total_ref.shape[0], 256, body)
    size = keep_ref.shape[1]
    for chip in range(2):
        for out_ref, mask in ((keep_ref, 2 * chip), (send_ref, 2 * chip + 1)):
            row = pl.multiple_of((at_ref[0] ^ mask) * size, size)
            out_ref[chip] = total_ref[pl.ds(row, size), :]


def make_terms(at, hidden, weight, scale):
    tokens, units = hidden.shape
    features = weight.shape[1]
    size = tokens // 4
    block = pl.BlockSpec((2, size, 512), lambda i, at: (0, 0, i))
    shape = jax.ShapeDtypeStruct((2, size, features), jnp.float32)
    return pl.pallas_call(
        functools.partial(terms_kernel, scale),
        grid_spec=pltpu.PrefetchScalarGridSpec(
            num_scalar_prefetch=1,
            grid=(features // 512,),
            in_specs=[
                pl.BlockSpec((tokens, units), lambda i, at: (0, 0)),
                pl.BlockSpec((units, 512), lambda i, at: (0, i)),
            ],
            out_specs=[block, block],
            scratch_shapes=[pltpu.VMEM((tokens, 512), jnp.float32)],
        ),
        out_shape=[shape, shape],
        compiler_params=params,
        cost_estimate=estimate(2 * units * tokens * features, units * features * 2 + tokens * features * 4),
    )(at, hidden, weight)


def chip_sum_kernel(keep_ref, sibling_ref, out_ref):
    def body(rows):
        out_ref[rows, :] = (keep_ref[0, rows, :] + sibling_ref[0, rows, :]).astype(out_ref.dtype)

    in_rows(out_ref.shape[0], 16, body)


def chip_sum(keep, sibling, kind):
    _, size, features = keep.shape
    block = pl.BlockSpec((1, size, features), lambda i: (1, 0, 0))
    return pl.pallas_call(
        chip_sum_kernel,
        grid=(1,),
        in_specs=[block, block],
        out_specs=pl.BlockSpec((size, features), lambda i: (0, 0)),
        out_shape=jax.ShapeDtypeStruct((size, features), kind),
        compiler_params=params,
        cost_estimate=estimate(size * features, size * features * 12),
    )(keep, sibling)


def last_sum_kernel(keep_ref, sibling_ref, other_ref, out_ref):
    def body(rows):
        total = keep_ref[0, rows, :] + sibling_ref[0, rows, :]
        out_ref[rows, :] = (total + other_ref[rows, :].astype(jnp.float32)).astype(jnp.bfloat16)

    in_rows(out_ref.shape[0], 16, body)


def last_sum(keep, sibling, other):
    _, size, features = keep.shape
    block = pl.BlockSpec((1, size, features), lambda i: (0, 0, 0))
    flat = pl.BlockSpec((size, features), lambda i: (0, 0))
    return pl.pallas_call(
        last_sum_kernel,
        grid=(1,),
        in_specs=[block, block, flat],
        out_specs=flat,
        out_shape=jax.ShapeDtypeStruct((size, features), jnp.bfloat16),
        compiler_params=params,
        cost_estimate=estimate(2 * size * features, size * features * 14),
    )(keep, sibling, other)


def grads_kernel(scale, at_ref, *refs):
    head_refs, rest_refs = refs[:4], refs[4:8]
    weight_ref, gate_ref, up_ref, gate_out, up_out, cot_ref, total_ref = refs[8:]

    @pl.when(pl.program_id(0) == 0)
    def _():
        put_tokens(at_ref, head_refs, cot_ref, 0)
        put_tokens(at_ref, rest_refs, cot_ref, head)

    def product(rows):
        total_ref[rows, :] = scale * lax.dot_general(
            cot_ref[rows, :], weight_ref[...], (((1,), (1,)), ((), ())), preferred_element_type=jnp.float32
        )

    in_rows(total_ref.shape[0], 256, product)

    def body(rows):
        total = total_ref[rows, :]
        gate = gate_ref[rows, :].astype(jnp.float32)
        up = up_ref[rows, :].astype(jnp.float32)
        sig = jax.nn.sigmoid(gate)
        gate_out[rows, :] = (total * up * sig * (1.0 + gate * (1.0 - sig))).astype(jnp.bfloat16)
        up_out[rows, :] = (total * (gate * sig)).astype(jnp.bfloat16)

    in_rows(gate_ref.shape[0], 64, body)


def make_grads(at, head_parts, rest_parts, weight, gate, up, scale):
    tokens, units = gate.shape
    features = weight.shape[1]
    wide = grads_wide
    block = pl.BlockSpec((tokens, wide), lambda i, at: (0, i))
    shape = jax.ShapeDtypeStruct((tokens, units), jnp.bfloat16)
    parts = list(head_parts) + list(rest_parts)
    return pl.pallas_call(
        functools.partial(grads_kernel, scale),
        grid_spec=pltpu.PrefetchScalarGridSpec(
            num_scalar_prefetch=1,
            grid=(units // wide,),
            in_specs=[pl.BlockSpec(part.shape, lambda i, at: (0, 0)) for part in parts]
            + [pl.BlockSpec((wide, features), lambda i, at: (i, 0)), block, block],
            out_specs=[block, block],
            scratch_shapes=[
                pltpu.VMEM((tokens, features), jnp.bfloat16),
                pltpu.VMEM((tokens, wide), jnp.float32),
            ],
        ),
        out_shape=[shape, shape],
        compiler_params=params,
        cost_estimate=estimate(2 * units * tokens * features, units * features * 2 + tokens * units * 8),
    )(at, *parts, weight, gate, up)


def averaged_kernel(own_ref, peer_ref, *refs):
    out_ref = refs[-1]

    def body(rows):
        own = own_ref[rows, :].astype(jnp.float32)
        out_ref[rows, :] = ((own + peer_ref[rows, :].astype(jnp.float32)) * 0.5).astype(jnp.bfloat16)

    in_rows(out_ref.shape[0], 64, body)


def averaged(mixed, own, peer, at, features):
    units, width = own.shape
    assert at % width == 0
    block = pl.BlockSpec((units // 2, width), lambda i: (i, 0))
    place_at = at // width
    before = [] if mixed is None else [mixed]
    return pl.pallas_call(
        averaged_kernel,
        grid=(2,),
        in_specs=[block, block] + [pl.BlockSpec(memory_space=pl.ANY)] * len(before),
        out_specs=pl.BlockSpec((units // 2, width), lambda i: (i, place_at)),
        out_shape=jax.ShapeDtypeStruct((units, features), jnp.bfloat16),
        input_output_aliases={2: 0} if before else {},
        compiler_params=params,
        cost_estimate=estimate(units * width * 2, units * width * 6),
    )(own, peer, *before)


def step_with(power, scale, at, gate, up, weight, head_parts, rest_rows, rest_core, hidden, new_head):
    features = weight.shape[1]
    factor = learning_rate * scale
    odd = power in (1, 3)
    rest_cuts = odd_cuts if odd else even_cuts
    around, order = ((2, 3), (0, 1, 4, 2, 5, 3, 6)) if odd else ((), (0, 1, 3, 4, 5, 2))

    def hop(value, piece, count):
        if piece in around:
            return lax.ppermute(value, both, backward_hops(power)[count])
        return lax.ppermute(value, both, direct_pairs(power))

    hops = {piece: hop(new_head[piece], piece, 0) for piece in ((0, 1, 2) if odd else (0, 1))}

    chip = swapped(rest_rows, 2)
    keep, send = make_terms(at, hidden, weight, scale)
    hops[0], chip, keep, send = lax.optimization_barrier((hops[0], chip, keep, send))
    if odd:
        hops[2], chip = lax.optimization_barrier((hops[2], chip))
        hops[2] = hop(hops[2], 2, 1)
    rest_parts = (rest_rows, rest_core, chip, swapped(chip, 1))

    new_rest = list(make_updated(at, rest_parts, hidden, weight, factor, head, rest_cuts))
    if odd:
        hops[3] = hop(new_rest[0], 3, 0)
        hops[4] = hop(new_rest[1], 4, 0)
        hops[1], hops[2], new_rest[2], gate, send = lax.optimization_barrier(
            (hops[1], hops[2], new_rest[2], gate, send)
        )
        hops[2] = hop(hops[2], 2, 2)
        hops[5] = hop(new_rest[2], 5, 0)
        hops[3] = hop(hops[3], 3, 1)
        hops[4], new_rest[3] = lax.optimization_barrier((hops[4], new_rest[3]))
        hops[6] = hop(new_rest[3], 6, 0)
        hops[2], hops[3] = lax.optimization_barrier((hops[2], hops[3]))
        hops[3] = hop(hops[3], 3, 2)
    else:
        hops[3] = hop(new_rest[0], 3, 0)
        hops[1], new_rest[1], send = lax.optimization_barrier((hops[1], new_rest[1], send))
        hops[4] = hop(new_rest[1], 4, 0)
        hops[3], new_rest[2], gate = lax.optimization_barrier((hops[3], new_rest[2], gate))
        hops[5] = hop(new_rest[2], 5, 0)
        hops[2] = hop(new_head[2], 2, 0)
    sibling = swapped(send, 1)
    grad_gate, grad_up = make_grads(at, head_parts, rest_parts, weight, gate, up, scale)
    kind = jnp.bfloat16 if power == 0 else jnp.float32
    layer_out = last_sum(keep, sibling, swapped(chip_sum(keep, sibling, kind), 2))

    pieces = list(new_head) + list(new_rest)
    starts = []
    column = 0
    for width in head_cuts + rest_cuts:
        starts.append(column)
        column += width
    mixed = None
    for count, piece in enumerate(order):
        value = hops[piece]
        if count == 3:
            value, layer_out = lax.optimization_barrier((value, layer_out))
        mixed = averaged(mixed, pieces[piece], value, starts[piece], features)
    return layer_out, grad_gate, grad_up, mixed


def per_device(gate_pre, up_pre, down_weight, cotangent, peer_exp):
    gate, up, weight, cot_rows = gate_pre[0], up_pre[0], down_weight[0], cotangent[0]
    width_all = weight.shape[0] * lax.axis_size("tensor")
    scale = float(np.float32(1.0) / np.sqrt(np.float32(width_all)))
    at = lax.axis_index("tensor").astype(jnp.int32).reshape(1)

    rows = cot_rows[:, :head]
    rest_rows = cot_rows[:, head:]
    core = swapped(rows, 1)
    chip = swapped(rows, 2)
    hidden = make_hidden(gate, up)
    chip, hidden, rest_rows = lax.optimization_barrier((chip, hidden, rest_rows))
    head_parts = (rows, core, chip, swapped(chip, 1))
    rest_core = swapped(rest_rows, 1)
    new_head = make_updated(at, head_parts, hidden, weight, learning_rate * scale, 0, head_cuts)

    outs = lax.switch(
        jnp.clip(peer_exp[0], 0, 4),
        [functools.partial(step_with, power, scale) for power in range(5)],
        at,
        gate,
        up,
        weight,
        head_parts,
        rest_rows,
        rest_core,
        hidden,
        tuple(new_head),
    )
    return tuple(out[None] for out in outs)


def solution(mesh):
    return jax.shard_map(
        per_device,
        mesh=mesh,
        in_specs=(
            P("replica", None, "tensor"),
            P("replica", None, "tensor"),
            P("replica", "tensor", None),
            P("replica", "tensor", None),
            P(),
        ),
        out_specs=(
            P("replica", "tensor", None),
            P("replica", None, "tensor"),
            P("replica", None, "tensor"),
            P("replica", "tensor", None),
        ),
        check_vma=False,
    )
```

time: 337 us -> 229 us (0.68); the launches traced: 337 us -> 225 us
  waiting for transfers between devices: 267 us -> 135 us
  Pallas kernels: 0 us -> 62.5 us
  matrix products: 36.1 us -> 0 us
  starting transfers between devices: 2.58 us -> 23 us
  between operations: 14.8 us -> 1.33 us
  other arithmetic: 12.3 us -> 0 us
    ppermute x1 -> x14, waiting for transfers between devices: 241 us -> 135 us  [the longest x6 126 us: hop(): return lax.ppermute(value, both, direct_pairs(power))]
    pallas_call x0 -> x13, Pallas kernels: none -> 62.5 us  [the longest x6 17.4 us: averaged(): pl.pallas_call(averaged_kernel, grid=(2,), in_specs=[block, block] + [pl....]
    dot_general x3 -> x0, matrix products: 36.1 us -> none  [the longest x1 12.9 us: contract_width(): lax.dot_general(left, right, (((1,), (1,)), ((), ())), preferred_element_...]
    all_gather x1 -> x0, waiting for transfers between devices: 25.8 us -> none  [per_device(): piece = lax.all_gather(cot_rows, 'tensor', axis=0, tiled=True)]
    ppermute x1 -> x14, starting transfers between devices: 2.5 us -> 23 us  [the longest x6 14 us: hop(): return lax.ppermute(value, both, direct_pairs(power))]
    broadcast_in_dim x2 -> x0, other arithmetic: 12.3 us -> none  [per_device(): return (layer_out[None], grad_gate[None], grad_up[None], mixed_weight[None])]
  transfers between devices with their start and end apart: 3 -> 14, of which waited for: 2 -> 10; matrix products, arithmetic and copies ran while one was open for 14% -> 0% of each run, Pallas kernels for 0% -> 27%
where the time goes in v1:
time: 229 us; the launch traced here: 225 us
  waiting for transfers between devices  135 us (59%)
  Pallas kernels  62.5 us (27%)
  starting transfers between devices  23 us (10%)
  local copies, waits for them, and re-layouts  3.38 us (1%)
    ppermute x6, waiting for transfers between devices, hop(): return lax.ppermute(value, both, direct_pairs(power))  126 us
    pallas_call x6, Pallas kernels, averaged(): pl.pallas_call(averaged_kernel, grid=(2,), in_specs=[block, block] + [pl....  17.4 us
    pallas_call x2, Pallas kernels, make_updated(): pl.pallas_call(functools.partial(updated_kernel, factor, first, cuts), gr...  14.3 us
    ppermute x6, starting transfers between devices, hop(): return lax.ppermute(value, both, direct_pairs(power))  14 us
    pallas_call x1, Pallas kernels, make_grads(): pl.pallas_call(functools.partial(grads_kernel, scale), grid_spec=pltpu.Pr...  12.5 us
    pallas_call x1, Pallas kernels, make_terms(): pl.pallas_call(functools.partial(terms_kernel, scale), grid_spec=pltpu.Pr...  10.3 us
    ppermute x8, starting transfers between devices, swapped(): return lax.ppermute(value, 'tensor', [(t, t ^ mask) for t in range(4)])  8.96 us
    ppermute x8, waiting for transfers between devices, swapped(): return lax.ppermute(value, 'tensor', [(t, t ^ mask) for t in range(4)])  8.91 us
  transfers between devices with their start and end apart: 14, of which 10 were waited for; matrix products, arithmetic and copies ran while one was open for 0% of the time, Pallas kernels for 27%

profile of v1, /device:TPU:1, one launch (start us, length us, event | category | flops | bytes accessed | tf_op | source)
XLA Modules:
  0.0 225.4 jit_solution(17106470838085747690)
XLA Ops:
  1.6 2.1 collective-permute-start.61
  3.7 2.6 %shard_map.84.hidden_ref = bf16[512,1792]{1,0:T(8,128)(2,1)S(1)} custom-call(bf16[512,1792]{1,0:T(8,128)(2,1)} %bitcast.25, bf16[512,1792]{1,0:T(8,128)(2,1)} %bitcast.31), custom_call_target="tpu_custom_call" | custom-call | flops 91750 | bytes 55050 | tf_op jit(solution)/shard_map/pallas_call | solution.py:79
  6.4 1.4 collective-permute-done.61.chip
  7.8 1.7 collective-permute-start.63
  11.6 4.5 %shard_map.85 = (bf16[1792,256]{1,0:T(8,128)(2,1)S(1)}, bf16[1792,256]{1,0:T(8,128)(2,1)}, bf16[1792,256]{1,0:T(8,128)(2,1)}) custom-call(s32[1]{0:T(128)} %bitcast.6.at_ref, bf16[128,768]{1,0:T(8,128)(2,1)S(1)} %slice.8.own, bf16[128,768]{1,0:T(8,128)(2,1)S(1)} %collective-permute-done.60.core, bf16[128,768]{1,0:T(8,128)(2,1)S(1)} %collective-permute-done.61.chip, ...), custom_call_target="tpu_custom_call" | custom-call | flops 14092861 | bytes 55050 | tf_op jit(solution)/shard_map/pallas_call | solution.py:123
  16.0 208.5 %conditional.1 = (bf16[128,2560]{1,0:T(8,128)(2,1)S(1)}, bf16[512,1792]{1,0:T(8,128)(2,1)}, bf16[512,1792]{1,0:T(8,128)(2,1)}, bf16[1,1792,2560]{2,1,0:T(8,128)(2,1)}) conditional(s32[]{:T(128)} %bitcast.5, (bf16[1792,256]{1,0:T(8,128)(2,1)}, bf16[1792,256]{1,0:T(8,128)(2,1)S(1)}, bf16[128,1792]{1,0:T(8,128)(2,1)S(1)}, ...), branch_computations={%region_0.1_spmd, %region_1.2_spmd, %region_2.3_spmd, %region_3.4_... | conditional | flops 126937344 | bytes 88120432 | solution.py:384
  16.6 3.2 %collective-permute-start.51 = (bf16[1792,256]{1,0:T(8,128)(2,1)S(1)}, bf16[1792,256]{1,0:T(8,128)(2,1)}, u32[]{:S(2)}, u32[]{:S(2)}) collective-permute-start(bf16[1792,256]{1,0:T(8,128)(2,1)S(1)} %get-tuple-element.289.own_ref), channel_id=1, source_target_pairs={{0,64},{1,65},{2,66},{3,67},{4,68},{5,69},{6,70},{7,71},{8,72},{9,... | collective-permute-start | bytes 2752520 | tf_op jit(solution)/shard_map/cond/branch_4_fun/ppermute | solution.py:315
  19.8 1.2 collective-permute-start.52
  21.0 10.3 %branch_4_fun.11 = (f32[2,128,2560]{2,1,0:T(8,128)}, f32[2,128,2560]{2,1,0:T(8,128)}) custom-call(s32[1]{0:T(128)} %get-tuple-element.286.at_ref, bf16[512,1792]{1,0:T(8,128)(2,1)S(1)} %get-tuple-element.290.hidden_ref, bf16[1792,2560]{1,0:T(8,128)(2,1)} %get-tuple-element.291.weight_ref.refs_8_), custom_call_target="tpu_custom_call" | custom-call | flops 46976204 | bytes 144179 | tf_op jit(solution)/shard_map/cond/branch_4_fun/pallas_call | solution.py:162
  31.3 8.9 %collective-permute-done.51.peer_ref = bf16[1792,256]{1,0:T(8,128)(2,1)} collective-permute-done((bf16[1792,256]{1,0:T(8,128)(2,1)S(1)}, bf16[1792,256]{1,0:T(8,128)(2,1)}, u32[]{:S(2)}, u32[]{:S(2)}) %collective-permute-start.51) | collective-permute-done | bytes 917536 | tf_op jit(solution)/shard_map/cond/branch_4_fun/ppermute | solution.py:315
  41.2 3.0 %collective-permute-start.50 = (bf16[1792,256]{1,0:T(8,128)(2,1)}, bf16[1792,256]{1,0:T(8,128)(2,1)}, u32[]{:S(2)}, u32[]{:S(2)}) collective-permute-start(bf16[1792,256]{1,0:T(8,128)(2,1)} %get-tuple-element.285.own_ref), channel_id=1, source_target_pairs={{0,64},{1,65},{2,66},{3,67},{4,68},{5,69},{6,70},{7,71},{8,72},{9,... | collective-permute-start | bytes 2752520 | tf_op jit(solution)/shard_map/cond/branch_4_fun/ppermute | solution.py:315
  44.2 9.9 %branch_4_fun.12 = (bf16[1792,768]{1,0:T(8,128)(2,1)}, bf16[1792,512]{1,0:T(8,128)(2,1)}, bf16[1792,512]{1,0:T(8,128)(2,1)}) custom-call(s32[1]{0:T(128)} %get-tuple-element.286.at_ref, bf16[128,1792]{1,0:T(8,128)(2,1)S(1)} %get-tuple-element.287.own.refs_4_, bf16[128,1792]{1,0:T(8,128)(2,1)S(1)} %get-tuple-element.288.core.refs_5_, ...), custom_call_target="tpu_custom_call" | custom-call | flops 32883344 | bytes 155975 | tf_op jit(solution)/shard_map/cond/branch_4_fun/pallas_call | solution.py:123
  54.1 1.8 collective-permute-start.57
  55.9 9.2 %collective-permute-done.50.peer_ref = bf16[1792,256]{1,0:T(8,128)(2,1)} collective-permute-done((bf16[1792,256]{1,0:T(8,128)(2,1)}, bf16[1792,256]{1,0:T(8,128)(2,1)}, u32[]{:S(2)}, u32[]{:S(2)}) %collective-permute-start.50) | collective-permute-done | bytes 917536 | tf_op jit(solution)/shard_map/cond/branch_4_fun/ppermute | solution.py:315
  65.0 1.2 collective-permute-start.55
  66.2 3.0 %collective-permute-start.54 = (bf16[1792,512]{1,0:T(8,128)(2,1)}, bf16[1792,512]{1,0:T(8,128)(2,1)}, u32[]{:S(2)}, u32[]{:S(2)}) collective-permute-start(bf16[1792,512]{1,0:T(8,128)(2,1)} %get-tuple-element.297.own_ref), channel_id=1, source_target_pairs={{0,64},{1,65},{2,66},{3,67},{4,68},{5,69},{6,70},{7,71},{8,72},{9,... | collective-permute-start | bytes 5505032 | tf_op jit(solution)/shard_map/cond/branch_4_fun/ppermute | solution.py:315
  69.2 54.7 %collective-permute-done.57.peer_ref = bf16[1792,768]{1,0:T(8,128)(2,1)S(1)} collective-permute-done((bf16[1792,768]{1,0:T(8,128)(2,1)}, bf16[1792,768]{1,0:T(8,128)(2,1)S(1)}, u32[]{:S(2)}, u32[]{:S(2)}) %collective-permute-start.57) | collective-permute-done | bytes 2752544 | tf_op jit(solution)/shard_map/cond/branch_4_fun/ppermute | solution.py:315
  123.9 1.5 copy-done.13
  125.5 3.0 %collective-permute-start.59 = (bf16[1792,512]{1,0:T(8,128)(2,1)}, bf16[1792,512]{1,0:T(8,128)(2,1)}, u32[]{:S(2)}, u32[]{:S(2)}) collective-permute-start(bf16[1792,512]{1,0:T(8,128)(2,1)} %get-tuple-element.313.own_ref), channel_id=1, source_target_pairs={{0,64},{1,65},{2,66},{3,67},{4,68},{5,69},{6,70},{7,71},{8,72},{9,... | collective-permute-start | bytes 5505032 | tf_op jit(solution)/shard_map/cond/branch_4_fun/ppermute | solution.py:315
  128.4 3.0 %branch_4_fun.13 = f32[128,2560]{1,0:T(8,128)} custom-call(f32[2,128,2560]{2,1,0:T(8,128)} %get-tuple-element.298.keep_ref, f32[2,128,2560]{2,1,0:T(8,128)} %collective-permute-done.55.sibling_ref), custom_call_target="tpu_custom_call" | custom-call | flops 3276 | bytes 39321 | tf_op jit(solution)/shard_map/cond/branch_4_fun/pallas_call | solution.py:190
  131.4 1.2 collective-permute-start.56
  132.7 2.3 %branch_4_fun.16.refs_0_ = bf16[1792,2560]{1,0:T(8,128)(2,1)} custom-call(bf16[1792,256]{1,0:T(8,128)(2,1)S(1)} %get-tuple-element.289.own_ref, bf16[1792,256]{1,0:T(8,128)(2,1)} %collective-permute-done.51.peer_ref), custom_call_target="tpu_custom_call" | custom-call | flops 9175 | bytes 27525 | tf_op jit(solution)/shard_map/cond/branch_4_fun/pallas_call | solution.py:293
  135.0 2.2 branch_4_fun.17.refs_0_
  137.2 4.1 %branch_4_fun.18.refs_0_ = bf16[1792,2560]{1,0:T(8,128)(2,1)} custom-call(bf16[1792,768]{1,0:T(8,128)(2,1)} %get-tuple-element.305.own_ref, bf16[1792,768]{1,0:T(8,128)(2,1)} %copy-done.13, bf16[1792,2560]{1,0:T(8,128)(2,1)} %branch_4_fun.17.refs_0_), custom_call_target="tpu_custom_call", output_to_operand_aliasing={{}: (2, {})} | custom-call | flops 27525 | bytes 82575 | tf_op jit(solution)/shard_map/cond/branch_4_fun/pallas_call | solution.py:293
  141.4 12.5 %branch_4_fun.15 = (bf16[512,1792]{1,0:T(8,128)(2,1)}, bf16[512,1792]{1,0:T(8,128)(2,1)}) custom-call(s32[1]{0:T(128)} %get-tuple-element.286.at_ref, bf16[128,768]{1,0:T(8,128)(2,1)S(1)} %get-tuple-element.301.refs_0_, bf16[128,768]{1,0:T(8,128)(2,1)S(1)} %get-tuple-element.302.refs_1_, bf16[128,768]{1,0:T(8,128)(2,1)S(1)} %get-tuple-element.303.refs_2_, ...), custom_call_target="tpu_custom_call" | custom-call | flops 46976204 | bytes 165150 | tf_op jit(solution)/shard_map/cond/branch_4_fun/pallas_call | solution.py:258
  153.9 6.6 %collective-permute-done.56.other_ref = f32[128,2560]{1,0:T(8,128)} collective-permute-done((f32[128,2560]{1,0:T(8,128)}, f32[128,2560]{1,0:T(8,128)}, u32[]{:S(2)}, u32[]{:S(2)}) %collective-permute-start.56) | collective-permute-done | bytes 1310752 | tf_op jit(solution)/shard_map/cond/branch_4_fun/ppermute | solution.py:52
  160.5 2.3 %branch_4_fun.14 = bf16[128,2560]{1,0:T(8,128)(2,1)S(1)} custom-call(f32[2,128,2560]{2,1,0:T(8,128)} %get-tuple-element.298.keep_ref, f32[2,128,2560]{2,1,0:T(8,128)} %collective-permute-done.55.sibling_ref, f32[128,2560]{1,0:T(8,128)} %collective-permute-done.56.other_ref), custom_call_target="tpu_custom_call" | custom-call | flops 6553 | bytes 45875 | tf_op jit(solution)/shard_map/cond/branch_4_fun/pallas_call | solution.py:213
  163.3 3.3 %branch_4_fun.19.refs_0_ = bf16[1792,2560]{1,0:T(8,128)(2,1)} custom-call(bf16[1792,512]{1,0:T(8,128)(2,1)} %get-tuple-element.297.own_ref, bf16[1792,512]{1,0:T(8,128)(2,1)} %collective-permute-done.54.peer_ref, bf16[1792,2560]{1,0:T(8,128)(2,1)} %branch_4_fun.18.refs_0_), custom_call_target="tpu_custom_call", output_to_operand_aliasing={{}: (2, {})} | custom-call | flops 18350 | bytes 55050 | tf_op jit(solution)/shard_map/cond/branch_4_fun/pallas_call | solution.py:293
  166.6 36.0 %collective-permute-done.59.peer_ref = bf16[1792,512]{1,0:T(8,128)(2,1)} collective-permute-done((bf16[1792,512]{1,0:T(8,128)(2,1)}, bf16[1792,512]{1,0:T(8,128)(2,1)}, u32[]{:S(2)}, u32[]{:S(2)}) %collective-permute-start.59) | collective-permute-done | bytes 1835040 | tf_op jit(solution)/shard_map/cond/branch_4_fun/ppermute | solution.py:315
  202.7 3.3 %branch_4_fun.20.refs_0_ = bf16[1792,2560]{1,0:T(8,128)(2,1)} custom-call(bf16[1792,512]{1,0:T(8,128)(2,1)} %get-tuple-element.313.own_ref, bf16[1792,512]{1,0:T(8,128)(2,1)} %collective-permute-done.59.peer_ref, bf16[1792,2560]{1,0:T(8,128)(2,1)} %branch_4_fun.19.refs_0_), custom_call_target="tpu_custom_call", output_to_operand_aliasing={{}: (2, {})} | custom-call | flops 18350 | bytes 55050 | tf_op jit(solution)/shard_map/cond/branch_4_fun/pallas_call | solution.py:293
  205.9 16.4 %collective-permute-done.58.peer_ref = bf16[1792,256]{1,0:T(8,128)(2,1)} collective-permute-done((bf16[1792,256]{1,0:T(8,128)(2,1)S(1)}, bf16[1792,256]{1,0:T(8,128)(2,1)}, u32[]{:S(2)}, u32[]{:S(2)}) %collective-permute-start.58) | collective-permute-done | bytes 917536 | tf_op jit(solution)/shard_map/cond/branch_4_fun/ppermute | solution.py:315
  222.3 2.2 branch_4_fun.21
  (26 shorter events, 4.8 us)
Async XLA Ops:
  1.6 6.2 %collective-permute-start.61 = (bf16[128,768]{1,0:T(8,128)(2,1)S(1)}, bf16[128,768]{1,0:T(8,128)(2,1)S(1)}, u32[]{:S(2)}, u32[]{:S(2)}) collective-permute-start(bf16[128,768]{1,0:T(8,128)(2,1)S(1)} %slice.8.own), channel_id=1, source_target_pairs={{0,2},{1,3},{2,0},{3,1},{4,6},{5,7},{6,4},{7,5},{8,10},{9,11},{10,... | collective-permute-start | bytes 589832 | tf_op jit(solution)/shard_map/ppermute | solution.py:52
  3.7 2.6 %copy-start.19 = (bf16[1,128,2560]{2,1,0:T(8,128)(2,1)S(1)}, bf16[1,128,2560]{2,1,0:T(8,128)(2,1)}, u32[]{:S(2)}) copy-start(bf16[1,128,2560]{2,1,0:T(8,128)(2,1)} %param.13) | copy-start | bytes 1966084
  7.8 8.2 %collective-permute-start.63 = (bf16[128,1792]{1,0:T(8,128)(2,1)S(1)}, bf16[128,1792]{1,0:T(8,128)(2,1)S(1)}, u32[]{:S(2)}, u32[]{:S(2)}) collective-permute-start(bf16[128,1792]{1,0:T(8,128)(2,1)S(1)} %slice.9), channel_id=1, source_target_pairs={{0,1},{1,0},{2,3},{3,2},{4,5},{5,4},{6,7},{7,6},{8,9},{9,8},{10,11... | collective-permute-start | bytes 1376264 | tf_op jit(solution)/shard_map/ppermute | solution.py:52
  9.6 1.7 collective-permute-start.60
  9.6 2.0 collective-permute-start.62
  11.6 4.5 %copy-start = (bf16[1,512,1792]{2,1,0:T(8,128)(2,1)S(1)}, bf16[1,512,1792]{2,1,0:T(8,128)(2,1)}, u32[]{:S(2)}) copy-start(bf16[1,512,1792]{2,1,0:T(8,128)(2,1)} %param.10) | copy-start | bytes 5505028
  11.6 4.5 %copy-start.1 = (bf16[1,512,1792]{2,1,0:T(8,128)(2,1)S(1)}, bf16[1,512,1792]{2,1,0:T(8,128)(2,1)}, u32[]{:S(2)}) copy-start(bf16[1,512,1792]{2,1,0:T(8,128)(2,1)} %param.11) | copy-start | bytes 5505028
  16.6 23.7 %collective-permute-start.51 = (bf16[1792,256]{1,0:T(8,128)(2,1)S(1)}, bf16[1792,256]{1,0:T(8,128)(2,1)}, u32[]{:S(2)}, u32[]{:S(2)}) collective-permute-start(bf16[1792,256]{1,0:T(8,128)(2,1)S(1)} %get-tuple-element.289.own_ref), channel_id=1, source_target_pairs={{0,64},{1,65},{2,66},{3,67},{4,68},{5,69},{6,70},{7,71},{8,72},{9,... | collective-permute-start | bytes 2752520 | tf_op jit(solution)/shard_map/cond/branch_4_fun/ppermute | solution.py:315
  19.8 11.5 %collective-permute-start.52 = (bf16[128,1792]{1,0:T(8,128)(2,1)S(1)}, bf16[128,1792]{1,0:T(8,128)(2,1)}, u32[]{:S(2)}, u32[]{:S(2)}) collective-permute-start(bf16[128,1792]{1,0:T(8,128)(2,1)S(1)} %get-tuple-element.287.own.refs_4_), channel_id=1, source_target_pairs={{0,2},{1,3},{2,0},{3,1},{4,6},{5,7},{6,4},{7,5},{8,10},{9,11},{10,... | collective-permute-start | bytes 1376264 | tf_op jit(solution)/shard_map/cond/branch_4_fun/ppermute | solution.py:52
  40.2 4.0 %collective-permute-start.53 = (bf16[128,1792]{1,0:T(8,128)(2,1)}, bf16[128,1792]{1,0:T(8,128)(2,1)}, u32[]{:S(2)}, u32[]{:S(2)}) collective-permute-start(bf16[128,1792]{1,0:T(8,128)(2,1)} %collective-permute-done.52.chip.refs_6_), channel_id=1, source_target_pairs={{0,1},{1,0},{2,3},{3,2},{4,5},{5,4},{6,7},{7,6},{8,9},{9,8},{10,11... | collective-permute-start | bytes 1376264 | tf_op jit(solution)/shard_map/cond/branch_4_fun/ppermute | solution.py:52
  41.2 23.8 %collective-permute-start.50 = (bf16[1792,256]{1,0:T(8,128)(2,1)}, bf16[1792,256]{1,0:T(8,128)(2,1)}, u32[]{:S(2)}, u32[]{:S(2)}) collective-permute-start(bf16[1792,256]{1,0:T(8,128)(2,1)} %get-tuple-element.285.own_ref), channel_id=1, source_target_pairs={{0,64},{1,65},{2,66},{3,67},{4,68},{5,69},{6,70},{7,71},{8,72},{9,... | collective-permute-start | bytes 2752520 | tf_op jit(solution)/shard_map/cond/branch_4_fun/ppermute | solution.py:315
  54.1 69.8 %collective-permute-start.57 = (bf16[1792,768]{1,0:T(8,128)(2,1)}, bf16[1792,768]{1,0:T(8,128)(2,1)S(1)}, u32[]{:S(2)}, u32[]{:S(2)}) collective-permute-start(bf16[1792,768]{1,0:T(8,128)(2,1)} %get-tuple-element.305.own_ref), channel_id=1, source_target_pairs={{0,64},{1,65},{2,66},{3,67},{4,68},{5,69},{6,70},{7,71},{8,72},{9,... | collective-permute-start | bytes 8257544 | tf_op jit(solution)/shard_map/cond/branch_4_fun/ppermute | solution.py:315
  65.0 63.4 %collective-permute-start.55 = (f32[2,128,2560]{2,1,0:T(8,128)}, f32[2,128,2560]{2,1,0:T(8,128)}, u32[]{:S(2)}, u32[]{:S(2)}) collective-permute-start(f32[2,128,2560]{2,1,0:T(8,128)} %get-tuple-element.299), channel_id=1, source_target_pairs={{0,1},{1,0},{2,3},{3,2},{4,5},{5,4},{6,7},{7,6},{8,9},{9,8},{10,11... | collective-permute-start | bytes 7864328 | tf_op jit(solution)/shard_map/cond/branch_4_fun/ppermute | solution.py:52
  66.2 97.1 %collective-permute-start.54 = (bf16[1792,512]{1,0:T(8,128)(2,1)}, bf16[1792,512]{1,0:T(8,128)(2,1)}, u32[]{:S(2)}, u32[]{:S(2)}) collective-permute-start(bf16[1792,512]{1,0:T(8,128)(2,1)} %get-tuple-element.297.own_ref), channel_id=1, source_target_pairs={{0,64},{1,65},{2,66},{3,67},{4,68},{5,69},{6,70},{7,71},{8,72},{9,... | collective-permute-start | bytes 5505032 | tf_op jit(solution)/shard_map/cond/branch_4_fun/ppermute | solution.py:315
  123.9 1.6 copy-start.13
  125.5 7.1 %copy-start.11 = (bf16[1792,256]{1,0:T(8,128)(2,1)S(1)}, bf16[1792,256]{1,0:T(8,128)(2,1)}, u32[]{:S(2)}) copy-start(bf16[1792,256]{1,0:T(8,128)(2,1)} %get-tuple-element.312.own_ref) | copy-start | bytes 2752516 | tf_op jit(solution)/shard_map/cond
  125.5 77.2 %collective-permute-start.59 = (bf16[1792,512]{1,0:T(8,128)(2,1)}, bf16[1792,512]{1,0:T(8,128)(2,1)}, u32[]{:S(2)}, u32[]{:S(2)}) collective-permute-start(bf16[1792,512]{1,0:T(8,128)(2,1)} %get-tuple-element.313.own_ref), channel_id=1, source_target_pairs={{0,64},{1,65},{2,66},{3,67},{4,68},{5,69},{6,70},{7,71},{8,72},{9,... | collective-permute-start | bytes 5505032 | tf_op jit(solution)/shard_map/cond/branch_4_fun/ppermute | solution.py:315
  131.4 29.1 %collective-permute-start.56 = (f32[128,2560]{1,0:T(8,128)}, f32[128,2560]{1,0:T(8,128)}, u32[]{:S(2)}, u32[]{:S(2)}) collective-permute-start(f32[128,2560]{1,0:T(8,128)} %branch_4_fun.13), channel_id=1, source_target_pairs={{0,2},{1,3},{2,0},{3,1},{4,6},{5,7},{6,4},{7,5},{8,10},{9,11},{10,... | collective-permute-start | bytes 3932168 | tf_op jit(solution)/shard_map/cond/branch_4_fun/ppermute | solution.py:52
  132.6 2.4 %copy-start.6 = (bf16[1792,256]{1,0:T(8,128)(2,1)S(1)}, bf16[1792,256]{1,0:T(8,128)(2,1)}, u32[]{:S(2)}) copy-start(bf16[1792,256]{1,0:T(8,128)(2,1)} %get-tuple-element.285.own_ref) | copy-start | bytes 2752516 | tf_op jit(solution)/shard_map/cond
  132.6 89.7 %collective-permute-start.58 = (bf16[1792,256]{1,0:T(8,128)(2,1)S(1)}, bf16[1792,256]{1,0:T(8,128)(2,1)}, u32[]{:S(2)}, u32[]{:S(2)}) collective-permute-start(bf16[1792,256]{1,0:T(8,128)(2,1)S(1)} %copy-done.11), channel_id=1, source_target_pairs={{0,64},{1,65},{2,66},{3,67},{4,68},{5,69},{6,70},{7,71},{8,72},{9,... | collective-permute-start | bytes 2752520 | tf_op jit(solution)/shard_map/cond/branch_4_fun/ppermute | solution.py:315
  224.5 0.8 copy-start.18

commit v2 on v1

--- a/solution.py
+++ b/solution.py
@@ -1,4 +1,5 @@
 import functools
+import math
 
 import jax
 import jax.numpy as jnp
@@ -12,9 +13,9 @@
 both = ("replica", "tensor")
 vmem = 56 * 2**20
 head = 768
-head_cuts = (256, 256, 256)
+head_runs = ((0, 512), (512, 256), (0, 256), (256, 256))
 even_cuts = (768, 512, 512)
-odd_cuts = (384, 384, 512, 512)
+odd_cuts = (384, 384, 1024)
 cost_cut = 100
 grads_wide = 256
 params = pltpu.CompilerParams(vmem_limit_bytes=vmem)
@@ -94,15 +95,21 @@
         whole_ref[pl.ds(row, size), lo : lo + wide] = part[...]
 
 
-def updated_kernel(factor, first, cuts, at_ref, own, core, chip, far, hidden_ref, weight_ref, *refs):
+def updated_kernel(factor, first, runs, at_ref, own, core, chip, far, hidden_ref, weight_ref, *refs):
     out_refs, cot_ref = refs[:-1], refs[-1]
 
     @pl.when(pl.program_id(0) == 0)
     def _():
         put_tokens(at_ref, (own, core, chip, far), cot_ref, 0)
 
-    at = 0
-    for out_ref, width in zip(out_refs, cuts):
+    made = []
+    for out_ref, (at, width) in zip(out_refs, runs):
+        inside = [(ref, at - lo) for ref, lo, size in made if lo <= at and at + width <= lo + size]
+        made.append((out_ref, at, width))
+        if inside:
+            wider, skip = inside[0]
+            out_ref[...] = wider[:, skip : skip + width]
+            continue
         total = lax.dot_general(
             hidden_ref[...],
             cot_ref[:, at : at + width],
@@ -111,17 +118,17 @@
         )
         old = weight_ref[:, first + at : first + at + width].astype(jnp.float32)
         out_ref[...] = (old - factor * total).astype(jnp.bfloat16)
-        at += width
-
-
-def make_updated(at, parts, hidden, weight, factor, first, cuts):
+
+
+def make_updated(at, parts, hidden, weight, factor, first, runs):
     tokens, units = hidden.shape
     rows = units // 2 if first == 0 else 256
-    wide = sum(cuts)
+    wide = parts[0].shape[1]
+    cuts = [width for _, width in runs]
     columns = wide if first == 0 else weight.shape[1]
     part = pl.BlockSpec(parts[0].shape, lambda i, at: (0, 0))
     return pl.pallas_call(
-        functools.partial(updated_kernel, factor, first, cuts),
+        functools.partial(updated_kernel, factor, first, runs),
         grid_spec=pltpu.PrefetchScalarGridSpec(
             num_scalar_prefetch=1,
             grid=(units // rows,),
@@ -286,15 +293,15 @@
 
 def averaged(mixed, own, peer, at, features):
     units, width = own.shape
-    assert at % width == 0
-    block = pl.BlockSpec((units // 2, width), lambda i: (i, 0))
-    place_at = at // width
+    run = math.gcd(width, at)
+    first = at // run
+    block = pl.BlockSpec((units // 2, run), lambda i, j: (i, j))
     before = [] if mixed is None else [mixed]
     return pl.pallas_call(
         averaged_kernel,
-        grid=(2,),
+        grid=(2, width // run),
         in_specs=[block, block] + [pl.BlockSpec(memory_space=pl.ANY)] * len(before),
-        out_specs=pl.BlockSpec((units // 2, width), lambda i: (i, place_at)),
+        out_specs=pl.BlockSpec((units // 2, run), lambda i, j: (i, first + j)),
         out_shape=jax.ShapeDtypeStruct((units, features), jnp.bfloat16),
         input_output_aliases={2: 0} if before else {},
         compiler_params=params,
@@ -306,62 +313,77 @@
     features = weight.shape[1]
     factor = learning_rate * scale
     odd = power in (1, 3)
-    rest_cuts = odd_cuts if odd else even_cuts
-    around, order = ((2, 3), (0, 1, 4, 2, 5, 3, 6)) if odd else ((), (0, 1, 3, 4, 5, 2))
+    if odd:
+        head_at, rest_cuts = ((0, 256), (256, 256), (512, 256)), odd_cuts
+        mine = [new_head[2], new_head[3], new_head[1]]
+        around, order = (2, 3), (0, 1, 2, 5, 4, 3)
+    else:
+        head_at, rest_cuts = ((0, 512), (512, 256)), even_cuts
+        mine = [new_head[0], new_head[1]]
+        around, order = (), (0, 2, 3, 4, 1)
+    rest_at, column = [], 0
+    for width in rest_cuts:
+        rest_at.append((column, width))
+        column += width
+    starts = [lo for lo, _ in head_at] + [head + lo for lo, _ in rest_at]
 
     def hop(value, piece, count):
         if piece in around:
             return lax.ppermute(value, both, backward_hops(power)[count])
         return lax.ppermute(value, both, direct_pairs(power))
 
-    hops = {piece: hop(new_head[piece], piece, 0) for piece in ((0, 1, 2) if odd else (0, 1))}
-
     chip = swapped(rest_rows, 2)
     keep, send = make_terms(at, hidden, weight, scale)
-    hops[0], chip, keep, send = lax.optimization_barrier((hops[0], chip, keep, send))
+    if power == 0:
+        mine[0], chip = lax.optimization_barrier((mine[0], chip))
+
+    hops = {0: hop(mine[0], 0, 0)}
+    chip, keep, send = lax.optimization_barrier((chip, keep, send))
     if odd:
-        hops[2], chip = lax.optimization_barrier((hops[2], chip))
+        hops[1] = hop(mine[1], 1, 0)
+        hops[2] = hop(mine[2], 2, 0)
+        hops[0], hops[2], chip = lax.optimization_barrier((hops[0], hops[2], chip))
         hops[2] = hop(hops[2], 2, 1)
     rest_parts = (rest_rows, rest_core, chip, swapped(chip, 1))
 
-    new_rest = list(make_updated(at, rest_parts, hidden, weight, factor, head, rest_cuts))
+    rest = list(make_updated(at, rest_parts, hidden, weight, factor, head, rest_at))
+    pieces = mine + rest
+    mixed = None
     if odd:
-        hops[3] = hop(new_rest[0], 3, 0)
-        hops[4] = hop(new_rest[1], 4, 0)
-        hops[1], hops[2], new_rest[2], gate, send = lax.optimization_barrier(
-            (hops[1], hops[2], new_rest[2], gate, send)
-        )
+        hops[3] = hop(rest[0], 3, 0)
+        hops[5] = hop(rest[2], 5, 0)
+        rest[1], gate = lax.optimization_barrier((rest[1], gate))
+        grad_gate, grad_up = make_grads(at, head_parts, rest_parts, weight, gate, up, scale)
+        hops[1], hops[2], rest[1], send = lax.optimization_barrier((hops[1], hops[2], rest[1], send))
         hops[2] = hop(hops[2], 2, 2)
-        hops[5] = hop(new_rest[2], 5, 0)
+        hops[4] = hop(rest[1], 4, 0)
+        sibling = swapped(send, 1)
+        summed = chip_sum(keep, sibling, jnp.float32)
+        hops[3], grad_gate = lax.optimization_barrier((hops[3], grad_gate))
         hops[3] = hop(hops[3], 3, 1)
-        hops[4], new_rest[3] = lax.optimization_barrier((hops[4], new_rest[3]))
-        hops[6] = hop(new_rest[3], 6, 0)
-        hops[2], hops[3] = lax.optimization_barrier((hops[2], hops[3]))
+        other = swapped(summed, 2)
+        for piece in order[:2]:
+            mixed = averaged(mixed, pieces[piece], hops[piece], starts[piece], features)
+        hops[2], hops[3], mixed, other = lax.optimization_barrier((hops[2], hops[3], mixed, other))
         hops[3] = hop(hops[3], 3, 2)
+        layer_out = last_sum(keep, sibling, other)
+        hops[5], layer_out = lax.optimization_barrier((hops[5], layer_out))
+        left = order[2:]
     else:
-        hops[3] = hop(new_rest[0], 3, 0)
-        hops[1], new_rest[1], send = lax.optimization_barrier((hops[1], new_rest[1], send))
-        hops[4] = hop(new_rest[1], 4, 0)
-        hops[3], new_rest[2], gate = lax.optimization_barrier((hops[3], new_rest[2], gate))
-        hops[5] = hop(new_rest[2], 5, 0)
-        hops[2] = hop(new_head[2], 2, 0)
-    sibling = swapped(send, 1)
-    grad_gate, grad_up = make_grads(at, head_parts, rest_parts, weight, gate, up, scale)
-    kind = jnp.bfloat16 if power == 0 else jnp.float32
-    layer_out = last_sum(keep, sibling, swapped(chip_sum(keep, sibling, kind), 2))
-
-    pieces = list(new_head) + list(new_rest)
-    starts = []
-    column = 0
-    for width in head_cuts + rest_cuts:
-        starts.append(column)
-        column += width
-    mixed = None
-    for count, piece in enumerate(order):
-        value = hops[piece]
-        if count == 3:
-            value, layer_out = lax.optimization_barrier((value, layer_out))
-        mixed = averaged(mixed, pieces[piece], value, starts[piece], features)
+        hops[2] = hop(rest[0], 2, 0)
+        hops[0], rest[1], send = lax.optimization_barrier((hops[0], rest[1], send))
+        hops[3] = hop(rest[1], 3, 0)
+        hops[2], rest[2], gate = lax.optimization_barrier((hops[2], rest[2], gate))
+        hops[4] = hop(rest[2], 4, 0)
+        hops[1] = hop(mine[1], 1, 0)
+        sibling = swapped(send, 1)
+        grad_gate, grad_up = make_grads(at, head_parts, rest_parts, weight, gate, up, scale)
+        kind = jnp.bfloat16 if power == 0 else jnp.float32
+        layer_out = last_sum(keep, sibling, swapped(chip_sum(keep, sibling, kind), 2))
+        hops[4], layer_out = lax.optimization_barrier((hops[4], layer_out))
+        left = order
+    for piece in left:
+        mixed = averaged(mixed, pieces[piece], hops[piece], starts[piece], features)
     return layer_out, grad_gate, grad_up, mixed
 
 
@@ -379,7 +401,7 @@
     chip, hidden, rest_rows = lax.optimization_barrier((chip, hidden, rest_rows))
     head_parts = (rows, core, chip, swapped(chip, 1))
     rest_core = swapped(rest_rows, 1)
-    new_head = make_updated(at, head_parts, hidden, weight, learning_rate * scale, 0, head_cuts)
+    new_head = make_updated(at, head_parts, hidden, weight, learning_rate * scale, 0, head_runs)
 
     outs = lax.switch(
         jnp.clip(peer_exp[0], 0, 4),

time: 229 us -> 187 us (0.82); the launches traced: 225 us -> 186 us
  waiting for transfers between devices: 135 us -> 89.1 us
  starting transfers between devices: 23 us -> 27.3 us
  Pallas kernels: 62.5 us -> 65 us
    ppermute x6 -> x4, waiting for transfers between devices: 126 us -> 27.6 us  [hop(): return lax.ppermute(value, both, direct_pairs(power))]
    ppermute x0 -> x6, waiting for transfers between devices: none -> 57.5 us  [hop(): return lax.ppermute(value, both, backward_hops(power)[count])]
    ppermute x0 -> x6, starting transfers between devices: none -> 14 us  [hop(): return lax.ppermute(value, both, backward_hops(power)[count])]
    ppermute x6 -> x4, starting transfers between devices: 14 us -> 3 us  [hop(): return lax.ppermute(value, both, direct_pairs(power))]
    ppermute x8, waiting for transfers between devices: 8.91 us -> 4.05 us  [swapped(): return lax.ppermute(value, 'tensor', [(t, t ^ mask) for t in range(4)])]
  transfers between devices with their start and end apart: 14 -> 18, of which waited for: 10 -> 10; matrix products, arithmetic and copies ran while one was open for 0% -> 0% of each run, Pallas kernels for 27% -> 33%
where the time goes in v2:
time: 187 us; the launch traced here: 186 us
  waiting for transfers between devices  89.1 us (48%)
  Pallas kernels  65 us (35%)
  starting transfers between devices  27.3 us (15%)
  local copies, waits for them, and re-layouts  3.17 us (2%)
    ppermute x6, waiting for transfers between devices, hop(): return lax.ppermute(value, both, backward_hops(power)[count])  57.5 us
    ppermute x4, waiting for transfers between devices, hop(): return lax.ppermute(value, both, direct_pairs(power))  27.6 us
    pallas_call x6, Pallas kernels, averaged(): pl.pallas_call(averaged_kernel, grid=(2, width // run), in_specs=[block,...  18.2 us
    pallas_call x2, Pallas kernels, make_updated(): pl.pallas_call(functools.partial(updated_kernel, factor, first, runs), gr...  15.2 us
    ppermute x6, starting transfers between devices, hop(): return lax.ppermute(value, both, backward_hops(power)[count])  14 us
    pallas_call x1, Pallas kernels, make_grads(): pl.pallas_call(functools.partial(grads_kernel, scale), grid_spec=pltpu.Pr...  12.5 us
    pallas_call x1, Pallas kernels, make_terms(): pl.pallas_call(functools.partial(terms_kernel, scale), grid_spec=pltpu.Pr...  10.3 us
    ppermute x8, starting transfers between devices, swapped(): return lax.ppermute(value, 'tensor', [(t, t ^ mask) for t in range(4)])  10.3 us
  transfers between devices with their start and end apart: 18, of which 10 were waited for; matrix products, arithmetic and copies ran while one was open for 0% of the time, Pallas kernels for 33%

profile of v2, /device:TPU:1, one launch (start us, length us, event | category | flops | bytes accessed | tf_op | source)
XLA Modules:
  0.0 186.3 jit_solution(15955644905376236379)
XLA Ops:
  1.6 2.1 %collective-permute-start.55 = (bf16[128,768]{1,0:T(8,128)(2,1)S(1)}, bf16[128,768]{1,0:T(8,128)(2,1)S(1)}, u32[]{:S(2)}, u32[]{:S(2)}) collective-permute-start(bf16[128,768]{1,0:T(8,128)(2,1)S(1)} %slice.8.own), channel_id=1, source_target_pairs={{0,2},{1,3},{2,0},{3,1},{4,6},{5,7},{6,4},{7,5},{8,10},{9,11},{10,... | collective-permute-start | bytes 589832 | tf_op jit(solution)/shard_map/ppermute | solution.py:53
  3.7 2.6 %shard_map.84.hidden_ref = bf16[512,1792]{1,0:T(8,128)(2,1)S(1)} custom-call(bf16[512,1792]{1,0:T(8,128)(2,1)} %bitcast.25, bf16[512,1792]{1,0:T(8,128)(2,1)} %bitcast.31), custom_call_target="tpu_custom_call" | custom-call | flops 91750 | bytes 55050 | tf_op jit(solution)/shard_map/pallas_call | solution.py:80
  6.4 1.4 collective-permute-done.55.chip
  7.8 1.7 collective-permute-start.58
  11.6 4.7 %shard_map.85 = (bf16[1792,512]{1,0:T(8,128)(2,1)}, bf16[1792,256]{1,0:T(8,128)(2,1)S(1)}, bf16[1792,256]{1,0:T(8,128)(2,1)}, bf16[1792,256]{1,0:T(8,128)(2,1)}) custom-call(s32[1]{0:T(128)} %bitcast.9.at_ref, bf16[128,768]{1,0:T(8,128)(2,1)S(1)} %slice.8.own, bf16[128,768]{1,0:T(8,128)(2,1)S(1)} %collective-permute-done.56.core, ...), custom_call_target="tpu_custom_call" | custom-call | flops 14092861 | bytes 55050 | tf_op jit(solution)/shard_map/pallas_call | solution.py:130
  16.3 170.0 %conditional.1 = (bf16[128,2560]{1,0:T(8,128)(2,1)}, bf16[512,1792]{1,0:T(8,128)(2,1)}, bf16[512,1792]{1,0:T(8,128)(2,1)}, bf16[1,1792,2560]{2,1,0:T(8,128)(2,1)}) conditional(s32[]{:T(128)} %bitcast.5, (bf16[128,1792]{1,0:T(8,128)(2,1)S(1)}, bf16[1792,512]{1,0:T(8,128)(2,1)}, s32[1]{0:T(128)}, ...), branch_computations={%region_0.1_spmd, %region_1.2_spmd, %region_2.3_spmd, %region_3.4_... | conditional | flops 126937344 | bytes 108043456 | solution.py:406
  16.5 1.6 collective-permute-start.32
  18.1 1.5 collective-permute-start.33
  20.9 10.3 %branch_3_fun.11 = (f32[2,128,2560]{2,1,0:T(8,128)}, f32[2,128,2560]{2,1,0:T(8,128)}) custom-call(s32[1]{0:T(128)} %get-tuple-element.240.at_ref, bf16[512,1792]{1,0:T(8,128)(2,1)S(1)} %get-tuple-element.245.hidden_ref, bf16[1792,2560]{1,0:T(8,128)(2,1)} %get-tuple-element.246.weight_ref.refs_8_), custom_call_target="tpu_custom_call" | custom-call | flops 46976204 | bytes 144179 | tf_op jit(solution)/shard_map/cond/branch_3_fun/pallas_call | solution.py:169
  31.2 9.1 %collective-permute-done.32.peer_ref = bf16[1792,256]{1,0:T(8,128)(2,1)} collective-permute-done((bf16[1792,256]{1,0:T(8,128)(2,1)}, bf16[1792,256]{1,0:T(8,128)(2,1)}, u32[]{:S(2)}, u32[]{:S(2)}) %collective-permute-start.32) | collective-permute-done | bytes 917536 | tf_op jit(solution)/shard_map/cond/branch_3_fun/ppermute | solution.py:333
  40.3 2.2 %collective-permute-start.38 = (bf16[1792,256]{1,0:T(8,128)(2,1)}, bf16[1792,256]{1,0:T(8,128)(2,1)}, u32[]{:S(2)}, u32[]{:S(2)}) collective-permute-start(bf16[1792,256]{1,0:T(8,128)(2,1)} %collective-permute-done.33), channel_id=1, source_target_pairs={{0,96},{1,97},{8,104},{9,105},{16,112},{17,113},{24,120},{25,121},... | collective-permute-start | bytes 2752520 | tf_op jit(solution)/shard_map/cond/branch_3_fun/ppermute | solution.py:332
  42.5 1.5 collective-permute-start.35
  44.0 1.8 collective-permute-done.35.far.refs_7_
  45.8 10.5 %branch_3_fun.12 = (bf16[1792,384]{1,0:T(8,128)(2,1)}, bf16[1792,384]{1,0:T(8,128)(2,1)}, bf16[1792,1024]{1,0:T(8,128)(2,1)}) custom-call(s32[1]{0:T(128)} %get-tuple-element.240.at_ref, bf16[128,1792]{1,0:T(8,128)(2,1)S(1)} %get-tuple-element.241.own.refs_4_, bf16[128,1792]{1,0:T(8,128)(2,1)S(1)} %get-tuple-element.242.core.refs_5_, ...), custom_call_target="tpu_custom_call" | custom-call | flops 32883344 | bytes 155975 | tf_op jit(solution)/shard_map/cond/branch_3_fun/pallas_call | solution.py:130
  56.3 3.6 %collective-permute-done.37.peer_ref = bf16[1792,256]{1,0:T(8,128)(2,1)} collective-permute-done((bf16[1792,256]{1,0:T(8,128)(2,1)}, bf16[1792,256]{1,0:T(8,128)(2,1)}, u32[]{:S(2)}, u32[]{:S(2)}) %collective-permute-start.37) | collective-permute-done | bytes 917536 | tf_op jit(solution)/shard_map/cond/branch_3_fun/ppermute | solution.py:333
  61.2 2.1 %collective-permute-start.39 = (f32[2,128,2560]{2,1,0:T(8,128)}, f32[2,128,2560]{2,1,0:T(8,128)}, u32[]{:S(2)}, u32[]{:S(2)}) collective-permute-start(f32[2,128,2560]{2,1,0:T(8,128)} %get-tuple-element.259), channel_id=1, source_target_pairs={{0,1},{1,0},{2,3},{3,2},{4,5},{5,4},{6,7},{7,6},{8,9},{9,8},{10,11... | collective-permute-start | bytes 7864328 | tf_op jit(solution)/shard_map/cond/branch_3_fun/ppermute | solution.py:53
  63.4 3.4 %collective-permute-start.41 = (bf16[1792,384]{1,0:T(8,128)(2,1)}, bf16[1792,384]{1,0:T(8,128)(2,1)}, u32[]{:S(2)}, u32[]{:S(2)}) collective-permute-start(bf16[1792,384]{1,0:T(8,128)(2,1)} %get-tuple-element.261.own_ref), channel_id=1, source_target_pairs={{0,96},{1,97},{8,104},{9,105},{16,112},{17,113},{24,120},{25,121},... | collective-permute-start | bytes 4128776 | tf_op jit(solution)/shard_map/cond/branch_3_fun/ppermute | solution.py:332
  66.8 12.5 %branch_3_fun.13 = (bf16[512,1792]{1,0:T(8,128)(2,1)}, bf16[512,1792]{1,0:T(8,128)(2,1)}) custom-call(s32[1]{0:T(128)} %get-tuple-element.240.at_ref, bf16[128,768]{1,0:T(8,128)(2,1)S(1)} %get-tuple-element.262.refs_0_, bf16[128,768]{1,0:T(8,128)(2,1)S(1)} %get-tuple-element.263.refs_1_, bf16[128,768]{1,0:T(8,128)(2,1)S(1)} %get-tuple-element.264.refs_2_, ...), custom_call_target="tpu_custom_call" | custom-call | flops 46976204 | bytes 165150 | tf_op jit(solution)/shard_map/cond/branch_3_fun/pallas_call | solution.py:265
  79.3 17.4 %collective-permute-done.41 = bf16[1792,384]{1,0:T(8,128)(2,1)} collective-permute-done((bf16[1792,384]{1,0:T(8,128)(2,1)}, bf16[1792,384]{1,0:T(8,128)(2,1)}, u32[]{:S(2)}, u32[]{:S(2)}) %collective-permute-start.41) | collective-permute-done | bytes 1376288 | tf_op jit(solution)/shard_map/cond/branch_3_fun/ppermute | solution.py:332
  96.7 3.4 %collective-permute-start.42 = (bf16[1792,384]{1,0:T(8,128)(2,1)}, bf16[1792,384]{1,0:T(8,128)(2,1)}, u32[]{:S(2)}, u32[]{:S(2)}) collective-permute-start(bf16[1792,384]{1,0:T(8,128)(2,1)} %collective-permute-done.41), channel_id=1, source_target_pairs={{0,96},{1,97},{8,104},{9,105},{16,112},{17,113},{24,120},{25,121},... | collective-permute-start | bytes 4128776 | tf_op jit(solution)/shard_map/cond/branch_3_fun/ppermute | solution.py:332
  100.1 3.0 %branch_3_fun.16 = f32[128,2560]{1,0:T(8,128)} custom-call(f32[2,128,2560]{2,1,0:T(8,128)} %get-tuple-element.252.keep_ref, f32[2,128,2560]{2,1,0:T(8,128)} %collective-permute-done.39.sibling_ref), custom_call_target="tpu_custom_call" | custom-call | flops 3276 | bytes 39321 | tf_op jit(solution)/shard_map/cond/branch_3_fun/pallas_call | solution.py:197
  104.3 2.2 %branch_3_fun.14.refs_0_ = bf16[1792,2560]{1,0:T(8,128)(2,1)} custom-call(bf16[1792,256]{1,0:T(8,128)(2,1)S(1)} %copy-done.6, bf16[1792,256]{1,0:T(8,128)(2,1)} %collective-permute-done.32.peer_ref), custom_call_target="tpu_custom_call" | custom-call | flops 9175 | bytes 27525 | tf_op jit(solution)/shard_map/cond/branch_3_fun/pallas_call | solution.py:300
  106.5 1.4 collective-permute-start.45
  107.9 2.2 %branch_3_fun.15.refs_0_ = bf16[1792,2560]{1,0:T(8,128)(2,1)} custom-call(bf16[1792,256]{1,0:T(8,128)(2,1)S(1)} %copy-done.8, bf16[1792,256]{1,0:T(8,128)(2,1)} %collective-permute-done.37.peer_ref, bf16[1792,2560]{1,0:T(8,128)(2,1)} %branch_3_fun.14.refs_0_), custom_call_target="tpu_custom_call", output_to_operand_aliasing={{}: (2, {})} | custom-call | flops 9175 | bytes 27525 | tf_op jit(solution)/shard_map/cond/branch_3_fun/pallas_call | solution.py:300
  110.1 38.7 %collective-permute-done.40.peer_ref = bf16[1792,256]{1,0:T(8,128)(2,1)S(1)} collective-permute-done((bf16[1792,256]{1,0:T(8,128)(2,1)}, bf16[1792,256]{1,0:T(8,128)(2,1)S(1)}, u32[]{:S(2)}, u32[]{:S(2)}) %collective-permute-start.40) | collective-permute-done | bytes 917536 | tf_op jit(solution)/shard_map/cond/branch_3_fun/ppermute | solution.py:332
  148.8 3.4 %collective-permute-start.44 = (bf16[1792,384]{1,0:T(8,128)(2,1)}, bf16[1792,384]{1,0:T(8,128)(2,1)S(1)}, u32[]{:S(2)}, u32[]{:S(2)}) collective-permute-start(bf16[1792,384]{1,0:T(8,128)(2,1)} %collective-permute-done.42), channel_id=1, source_target_pairs={{0,96},{1,97},{8,104},{9,105},{16,112},{17,113},{24,120},{25,121},... | collective-permute-start | bytes 4128776 | tf_op jit(solution)/shard_map/cond/branch_3_fun/ppermute | solution.py:332
  152.2 3.2 %branch_3_fun.17 = bf16[128,2560]{1,0:T(8,128)(2,1)} custom-call(f32[2,128,2560]{2,1,0:T(8,128)} %get-tuple-element.252.keep_ref, f32[2,128,2560]{2,1,0:T(8,128)} %collective-permute-done.39.sibling_ref, f32[128,2560]{1,0:T(8,128)} %copy-done.20), custom_call_target="tpu_custom_call" | custom-call | flops 6553 | bytes 45875 | tf_op jit(solution)/shard_map/cond/branch_3_fun/pallas_call | solution.py:220
  155.4 2.2 %branch_3_fun.18.refs_0_ = bf16[1792,2560]{1,0:T(8,128)(2,1)} custom-call(bf16[1792,256]{1,0:T(8,128)(2,1)S(1)} %get-tuple-element.244.own_ref, bf16[1792,256]{1,0:T(8,128)(2,1)} %copy-done.22, bf16[1792,2560]{1,0:T(8,128)(2,1)} %branch_3_fun.15.refs_0_), custom_call_target="tpu_custom_call", output_to_operand_aliasing={{}: (2, {})} | custom-call | flops 9175 | bytes 27525 | tf_op jit(solution)/shard_map/cond/branch_3_fun/pallas_call | solution.py:300
  157.6 5.8 %branch_3_fun.19.refs_0_ = bf16[1792,2560]{1,0:T(8,128)(2,1)} custom-call(bf16[1792,1024]{1,0:T(8,128)(2,1)} %get-tuple-element.251.own_ref, bf16[1792,1024]{1,0:T(8,128)(2,1)} %collective-permute-done.36.peer_ref, bf16[1792,2560]{1,0:T(8,128)(2,1)} %branch_3_fun.18.refs_0_), custom_call_target="tpu_custom_call", output_to_operand_aliasing={{}: (2, {})} | custom-call | flops 36700 | bytes 110100 | tf_op jit(solution)/shard_map/cond/branch_3_fun/pallas_call | solution.py:300
  163.5 14.9 %collective-permute-done.45.peer_ref = bf16[1792,384]{1,0:T(8,128)(2,1)S(1)} collective-permute-done((bf16[1792,384]{1,0:T(8,128)(2,1)S(1)}, bf16[1792,384]{1,0:T(8,128)(2,1)S(1)}, u32[]{:S(2)}, u32[]{:S(2)}) %collective-permute-start.45) | collective-permute-done | bytes 1376288 | tf_op jit(solution)/shard_map/cond/branch_3_fun/ppermute | solution.py:333
  179.4 2.9 %branch_3_fun.20.refs_0_ = bf16[1792,2560]{1,0:T(8,128)(2,1)} custom-call(bf16[1792,384]{1,0:T(8,128)(2,1)} %get-tuple-element.277.own_ref, bf16[1792,384]{1,0:T(8,128)(2,1)} %copy-done.16, bf16[1792,2560]{1,0:T(8,128)(2,1)} %branch_3_fun.19.refs_0_), custom_call_target="tpu_custom_call", output_to_operand_aliasing={{}: (2, {})} | custom-call | flops 13762 | bytes 41287 | tf_op jit(solution)/shard_map/cond/branch_3_fun/pallas_call | solution.py:300
  183.4 2.9 %branch_3_fun.21 = bf16[1792,2560]{1,0:T(8,128)(2,1)} custom-call(bf16[1792,384]{1,0:T(8,128)(2,1)} %get-tuple-element.261.own_ref, bf16[1792,384]{1,0:T(8,128)(2,1)} %copy-done.18, bf16[1792,2560]{1,0:T(8,128)(2,1)} %branch_3_fun.20.refs_0_), custom_call_target="tpu_custom_call", output_to_operand_aliasing={{}: (2, {})} | custom-call | flops 13762 | bytes 41287 | tf_op jit(solution)/shard_map/cond/branch_3_fun/pallas_call | solution.py:300
  (40 shorter events, 8.2 us)
Async XLA Ops:
  1.6 6.2 %collective-permute-start.55 = (bf16[128,768]{1,0:T(8,128)(2,1)S(1)}, bf16[128,768]{1,0:T(8,128)(2,1)S(1)}, u32[]{:S(2)}, u32[]{:S(2)}) collective-permute-start(bf16[128,768]{1,0:T(8,128)(2,1)S(1)} %slice.8.own), channel_id=1, source_target_pairs={{0,2},{1,3},{2,0},{3,1},{4,6},{5,7},{6,4},{7,5},{8,10},{9,11},{10,... | collective-permute-start | bytes 589832 | tf_op jit(solution)/shard_map/ppermute | solution.py:53
  3.7 2.6 %copy-start.23 = (bf16[1,128,2560]{2,1,0:T(8,128)(2,1)S(1)}, bf16[1,128,2560]{2,1,0:T(8,128)(2,1)}, u32[]{:S(2)}) copy-start(bf16[1,128,2560]{2,1,0:T(8,128)(2,1)} %param.13) | copy-start | bytes 1966084
  7.8 8.4 %collective-permute-start.58 = (bf16[128,1792]{1,0:T(8,128)(2,1)S(1)}, bf16[128,1792]{1,0:T(8,128)(2,1)S(1)}, u32[]{:S(2)}, u32[]{:S(2)}) collective-permute-start(bf16[128,1792]{1,0:T(8,128)(2,1)S(1)} %slice.9), channel_id=1, source_target_pairs={{0,1},{1,0},{2,3},{3,2},{4,5},{5,4},{6,7},{7,6},{8,9},{9,8},{10,11... | collective-permute-start | bytes 1376264 | tf_op jit(solution)/shard_map/ppermute | solution.py:53
  9.6 1.7 collective-permute-start.56
  9.6 2.0 %collective-permute-start.57 = (bf16[128,768]{1,0:T(8,128)(2,1)S(1)}, bf16[128,768]{1,0:T(8,128)(2,1)S(1)}, u32[]{:S(2)}, u32[]{:S(2)}) collective-permute-start(bf16[128,768]{1,0:T(8,128)(2,1)S(1)} %collective-permute-done.55.chip), channel_id=1, source_target_pairs={{0,1},{1,0},{2,3},{3,2},{4,5},{5,4},{6,7},{7,6},{8,9},{9,8},{10,11... | collective-permute-start | bytes 589832 | tf_op jit(solution)/shard_map/ppermute | solution.py:53
  11.6 4.7 %copy-start = (bf16[1,512,1792]{2,1,0:T(8,128)(2,1)S(1)}, bf16[1,512,1792]{2,1,0:T(8,128)(2,1)}, u32[]{:S(2)}) copy-start(bf16[1,512,1792]{2,1,0:T(8,128)(2,1)} %param.10) | copy-start | bytes 5505028
  11.6 4.7 %copy-start.1 = (bf16[1,512,1792]{2,1,0:T(8,128)(2,1)S(1)}, bf16[1,512,1792]{2,1,0:T(8,128)(2,1)}, u32[]{:S(2)}) copy-start(bf16[1,512,1792]{2,1,0:T(8,128)(2,1)} %param.11) | copy-start | bytes 5505028
  16.5 23.8 %collective-permute-start.32 = (bf16[1792,256]{1,0:T(8,128)(2,1)}, bf16[1792,256]{1,0:T(8,128)(2,1)}, u32[]{:S(2)}, u32[]{:S(2)}) collective-permute-start(bf16[1792,256]{1,0:T(8,128)(2,1)} %get-tuple-element.243.own_ref), channel_id=1, source_target_pairs={{0,32},{1,33},{2,34},{3,35},{4,36},{5,37},{6,38},{7,39},{8,40},{9,... | collective-permute-start | bytes 2752520 | tf_op jit(solution)/shard_map/cond/branch_3_fun/ppermute | solution.py:333
  18.1 22.2 %collective-permute-start.33 = (bf16[1792,256]{1,0:T(8,128)(2,1)S(1)}, bf16[1792,256]{1,0:T(8,128)(2,1)}, u32[]{:S(2)}, u32[]{:S(2)}) collective-permute-start(bf16[1792,256]{1,0:T(8,128)(2,1)S(1)} %get-tuple-element.244.own_ref), channel_id=1, source_target_pairs={{0,96},{1,97},{8,104},{9,105},{16,112},{17,113},{24,120},{25,121},... | collective-permute-start | bytes 2752520 | tf_op jit(solution)/shard_map/cond/branch_3_fun/ppermute | solution.py:332
  19.6 11.5 %collective-permute-start.34 = (bf16[128,1792]{1,0:T(8,128)(2,1)S(1)}, bf16[128,1792]{1,0:T(8,128)(2,1)}, u32[]{:S(2)}, u32[]{:S(2)}) collective-permute-start(bf16[128,1792]{1,0:T(8,128)(2,1)S(1)} %get-tuple-element.241.own.refs_4_), channel_id=1, source_target_pairs={{0,2},{1,3},{2,0},{3,1},{4,6},{5,7},{6,4},{7,5},{8,10},{9,11},{10,... | collective-permute-start | bytes 1376264 | tf_op jit(solution)/shard_map/cond/branch_3_fun/ppermute | solution.py:53
  20.9 39.1 %collective-permute-start.37 = (bf16[1792,256]{1,0:T(8,128)(2,1)}, bf16[1792,256]{1,0:T(8,128)(2,1)}, u32[]{:S(2)}, u32[]{:S(2)}) collective-permute-start(bf16[1792,256]{1,0:T(8,128)(2,1)} %get-tuple-element.253.own_ref), channel_id=1, source_target_pairs={{0,32},{1,33},{2,34},{3,35},{4,36},{5,37},{6,38},{7,39},{8,40},{9,... | collective-permute-start | bytes 2752520 | tf_op jit(solution)/shard_map/cond/branch_3_fun/ppermute | solution.py:333
  40.3 21.0 %collective-permute-start.38 = (bf16[1792,256]{1,0:T(8,128)(2,1)}, bf16[1792,256]{1,0:T(8,128)(2,1)}, u32[]{:S(2)}, u32[]{:S(2)}) collective-permute-start(bf16[1792,256]{1,0:T(8,128)(2,1)} %collective-permute-done.33), channel_id=1, source_target_pairs={{0,96},{1,97},{8,104},{9,105},{16,112},{17,113},{24,120},{25,121},... | collective-permute-start | bytes 2752520 | tf_op jit(solution)/shard_map/cond/branch_3_fun/ppermute | solution.py:332
  42.5 3.3 %collective-permute-start.35 = (bf16[128,1792]{1,0:T(8,128)(2,1)}, bf16[128,1792]{1,0:T(8,128)(2,1)}, u32[]{:S(2)}, u32[]{:S(2)}) collective-permute-start(bf16[128,1792]{1,0:T(8,128)(2,1)} %collective-permute-done.34.chip.refs_6_), channel_id=1, source_target_pairs={{0,1},{1,0},{2,3},{3,2},{4,5},{5,4},{6,7},{7,6},{8,9},{9,8},{10,11... | collective-permute-start | bytes 1376264 | tf_op jit(solution)/shard_map/cond/branch_3_fun/ppermute | solution.py:53
  61.2 38.9 %collective-permute-start.39 = (f32[2,128,2560]{2,1,0:T(8,128)}, f32[2,128,2560]{2,1,0:T(8,128)}, u32[]{:S(2)}, u32[]{:S(2)}) collective-permute-start(f32[2,128,2560]{2,1,0:T(8,128)} %get-tuple-element.259), channel_id=1, source_target_pairs={{0,1},{1,0},{2,3},{3,2},{4,5},{5,4},{6,7},{7,6},{8,9},{9,8},{10,11... | collective-permute-start | bytes 7864328 | tf_op jit(solution)/shard_map/cond/branch_3_fun/ppermute | solution.py:53
  63.4 33.3 %collective-permute-start.41 = (bf16[1792,384]{1,0:T(8,128)(2,1)}, bf16[1792,384]{1,0:T(8,128)(2,1)}, u32[]{:S(2)}, u32[]{:S(2)}) collective-permute-start(bf16[1792,384]{1,0:T(8,128)(2,1)} %get-tuple-element.261.own_ref), channel_id=1, source_target_pairs={{0,96},{1,97},{8,104},{9,105},{16,112},{17,113},{24,120},{25,121},... | collective-permute-start | bytes 4128776 | tf_op jit(solution)/shard_map/cond/branch_3_fun/ppermute | solution.py:332
  66.8 90.8 %collective-permute-start.36 = (bf16[1792,1024]{1,0:T(8,128)(2,1)}, bf16[1792,1024]{1,0:T(8,128)(2,1)}, u32[]{:S(2)}, u32[]{:S(2)}) collective-permute-start(bf16[1792,1024]{1,0:T(8,128)(2,1)} %get-tuple-element.251.own_ref), channel_id=1, source_target_pairs={{0,32},{1,33},{2,34},{3,35},{4,36},{5,37},{6,38},{7,39},{8,40},{9,... | collective-permute-start | bytes 11010056 | tf_op jit(solution)/shard_map/cond/branch_3_fun/ppermute | solution.py:333
  96.7 7.6 %copy-start.6 = (bf16[1792,256]{1,0:T(8,128)(2,1)S(1)}, bf16[1792,256]{1,0:T(8,128)(2,1)}, u32[]{:S(2)}) copy-start(bf16[1792,256]{1,0:T(8,128)(2,1)} %get-tuple-element.243.own_ref) | copy-start | bytes 2752516 | tf_op jit(solution)/shard_map/cond
  96.7 52.1 %collective-permute-start.42 = (bf16[1792,384]{1,0:T(8,128)(2,1)}, bf16[1792,384]{1,0:T(8,128)(2,1)}, u32[]{:S(2)}, u32[]{:S(2)}) collective-permute-start(bf16[1792,384]{1,0:T(8,128)(2,1)} %collective-permute-done.41), channel_id=1, source_target_pairs={{0,96},{1,97},{8,104},{9,105},{16,112},{17,113},{24,120},{25,121},... | collective-permute-start | bytes 4128776 | tf_op jit(solution)/shard_map/cond/branch_3_fun/ppermute | solution.py:332
  103.1 3.4 %copy-start.14 = (bf16[1792,384]{1,0:T(8,128)(2,1)S(1)}, bf16[1792,384]{1,0:T(8,128)(2,1)}, u32[]{:S(2)}) copy-start(bf16[1792,384]{1,0:T(8,128)(2,1)} %get-tuple-element.277.own_ref) | copy-start | bytes 4128772 | tf_op jit(solution)/shard_map/cond
  103.1 4.8 %copy-start.8 = (bf16[1792,256]{1,0:T(8,128)(2,1)S(1)}, bf16[1792,256]{1,0:T(8,128)(2,1)}, u32[]{:S(2)}) copy-start(bf16[1792,256]{1,0:T(8,128)(2,1)} %get-tuple-element.253.own_ref) | copy-start | bytes 2752516 | tf_op jit(solution)/shard_map/cond
  103.1 45.7 %collective-permute-start.43 = (f32[128,2560]{1,0:T(8,128)}, f32[128,2560]{1,0:T(8,128)S(1)}, u32[]{:S(2)}, u32[]{:S(2)}) collective-permute-start(f32[128,2560]{1,0:T(8,128)} %branch_3_fun.16), channel_id=1, source_target_pairs={{0,2},{1,3},{2,0},{3,1},{4,6},{5,7},{6,4},{7,5},{8,10},{9,11},{10,... | collective-permute-start | bytes 3932168 | tf_op jit(solution)/shard_map/cond/branch_3_fun/ppermute | solution.py:53
  104.2 44.6 %collective-permute-start.40 = (bf16[1792,256]{1,0:T(8,128)(2,1)}, bf16[1792,256]{1,0:T(8,128)(2,1)S(1)}, u32[]{:S(2)}, u32[]{:S(2)}) collective-permute-start(bf16[1792,256]{1,0:T(8,128)(2,1)} %collective-permute-done.38), channel_id=1, source_target_pairs={{0,96},{1,97},{8,104},{9,105},{16,112},{17,113},{24,120},{25,121},... | collective-permute-start | bytes 2752520 | tf_op jit(solution)/shard_map/cond/branch_3_fun/ppermute | solution.py:332
  106.5 71.8 %collective-permute-start.45 = (bf16[1792,384]{1,0:T(8,128)(2,1)S(1)}, bf16[1792,384]{1,0:T(8,128)(2,1)S(1)}, u32[]{:S(2)}, u32[]{:S(2)}) collective-permute-start(bf16[1792,384]{1,0:T(8,128)(2,1)S(1)} %copy-done.14), channel_id=1, source_target_pairs={{0,32},{1,33},{2,34},{3,35},{4,36},{5,37},{6,38},{7,39},{8,40},{9,... | collective-permute-start | bytes 4128776 | tf_op jit(solution)/shard_map/cond/branch_3_fun/ppermute | solution.py:333
  148.8 6.6 %copy-start.22 = (bf16[1792,256]{1,0:T(8,128)(2,1)}, bf16[1792,256]{1,0:T(8,128)(2,1)S(1)}, u32[]{:S(2)}) copy-start(bf16[1792,256]{1,0:T(8,128)(2,1)S(1)} %collective-permute-done.40.peer_ref) | copy-start | bytes 2752516 | tf_op jit(solution)/shard_map/cond
  148.8 3.4 %copy-start.20 = (f32[128,2560]{1,0:T(8,128)}, f32[128,2560]{1,0:T(8,128)S(1)}, u32[]{:S(2)}) copy-start(f32[128,2560]{1,0:T(8,128)S(1)} %collective-permute-done.43.other_ref) | copy-start | bytes 3932164 | tf_op jit(solution)/shard_map/cond
  148.8 33.5 %collective-permute-start.44 = (bf16[1792,384]{1,0:T(8,128)(2,1)}, bf16[1792,384]{1,0:T(8,128)(2,1)S(1)}, u32[]{:S(2)}, u32[]{:S(2)}) collective-permute-start(bf16[1792,384]{1,0:T(8,128)(2,1)} %collective-permute-done.42), channel_id=1, source_target_pairs={{0,96},{1,97},{8,104},{9,105},{16,112},{17,113},{24,120},{25,121},... | collective-permute-start | bytes 4128776 | tf_op jit(solution)/shard_map/cond/branch_3_fun/ppermute | solution.py:332
  178.4 1.1 copy-start.16
  182.3 1.1 copy-start.18
